TPU v7x, 32 devices: a whole 2x2x4 slice. The times are simulated.
32 devices in a mesh: dp: 4 (over x, core), seq: 4 (over z), tensor: 2 (over y).
Axes of the slice: x: 2, y: 2, z: 4, core: 2. Of those that a mesh axis runs over, the one named last changes fastest.
Arguments:
- byte_acts: bfloat16 [4, 16384, 2048], P('dp', 'seq', 'tensor'), may hold values from -18 to 18
- conv_weight: bfloat16 [16, 1024, 128], P('tensor'), may hold values from -0.1875 to 0.1875
- conv_bias: float32 [2048], P('tensor'), may hold values from -3 to 3
- proj_weight: bfloat16 [2048, 8192], P(None, 'tensor'), may hold values from -0.125 to 0.125
- teacher: bfloat16 [4, 4096, 8192], P('dp', 'seq', 'tensor'), may hold values from -6 to 6
- span_lengths: int32 [4, 4096], P('dp'), may hold values from 1 to 16, as said below
Outputs:
- downsampled: bfloat16 [4, 4096, 2048], P('dp', 'seq', 'tensor')
- byte_grad: bfloat16 [4, 16384, 2048], P('dp', 'seq', 'tensor')
- conv_grad: float32 [16, 1024, 128], P('tensor')
- proj_grad: float32 [2048, 8192], P(None, 'tensor')
Inputs may be any that keep to these rules, and one draw needn't show every extreme that they name: `span_lengths`: each document's 4096 span lengths cover its 16384 bytes in order; the longest is exactly 16.
All inputs are finite; a program needn't handle non-finite values.
Results may differ from a plain program's by a relative error of at most 0.019.
Values may be sent and summed in bfloat16 or wider, within the bound.
A program may use at most 256 MiB of HBM per device.

v0:
```python
import jax
import jax.numpy as jnp
from jax import lax
from jax.sharding import PartitionSpec as P

STRIDE = 4
KERNEL = 8


def shifted(block, axis, distance):
    devices = range(lax.axis_size(axis))
    route = [(i - distance, i) for i in devices if i - distance in devices]
    return lax.ppermute(block, axis, route)


def intersection_weights(span_start, span_end, span_lengths, first_position, position_count):
    byte_first = (first_position + jnp.arange(position_count, dtype=jnp.int32)) * STRIDE
    lower_edge = jnp.maximum(span_start[:, None], byte_first[None, :])
    upper_edge = jnp.minimum(span_end[:, None], byte_first[None, :] + STRIDE)
    covered = jnp.maximum(upper_edge - lower_edge, 0).astype(jnp.float32)
    return (covered / span_lengths[:, None].astype(jnp.float32)).astype(jnp.bfloat16)


def local(byte_acts, conv_weight, conv_bias, proj_weight, teacher, span_lengths):
    byte_rows = byte_acts[0]
    row_total, width = byte_rows.shape
    groups_here = conv_weight.shape[0]
    group_width = width // groups_here
    positions = row_total // STRIDE
    seq_count = lax.axis_size("seq")
    seq_rank = lax.axis_index("seq")
    lengths_doc = span_lengths[0]
    tokens_all = lengths_doc.shape[0]
    span_end = jnp.cumsum(lengths_doc)
    span_start = span_end - lengths_doc
    next_rows = shifted(byte_rows[:STRIDE], "seq", -1)
    extended = jnp.concatenate([byte_rows, next_rows], axis=0)
    blocks = extended.reshape(positions + 1, STRIDE, groups_here, group_width)
    windows = jnp.concatenate([blocks[:-1], blocks[1:]], axis=1)
    taps_weight = conv_weight.reshape(groups_here, KERNEL, group_width, group_width)
    conv_out = jnp.einsum(
        "pkgc,gkco->pgo", windows, taps_weight, preferred_element_type=jnp.float32
    )
    conv_out = conv_out + conv_bias.reshape(groups_here, group_width)[None]
    downsampled = conv_out.reshape(positions, width).astype(jnp.bfloat16)
    local_weight = intersection_weights(
        span_start, span_end, lengths_doc, seq_rank * positions, positions
    )
    weight_part = local_weight
    pooled_sum = lax.psum_scatter(
        jnp.dot(weight_part, downsampled, preferred_element_type=jnp.float32).astype(jnp.bfloat16),
        "seq",
        scatter_dimension=0,
        tiled=True,
    )
    gathered = lax.all_gather(pooled_sum, "tensor", axis=1, tiled=True)
    predicted = jnp.dot(gathered, proj_weight, preferred_element_type=jnp.float32)
    err_grad = (predicted - teacher[0].astype(jnp.float32)).astype(jnp.bfloat16)
    proj_local = lax.dot_general(
        gathered, err_grad, (((0,), (0,)), ((), ())), preferred_element_type=jnp.float32
    )
    token_scale = 1.0 / jnp.sqrt(jnp.float32(lax.axis_size("dp") * tokens_all))
    proj_summed = lax.psum(proj_local.astype(jnp.bfloat16), ("dp", "seq")).astype(jnp.float32)
    proj_grad = proj_summed * token_scale
    weight_part = proj_weight
    pooled_grad_t = lax.psum_scatter(
        lax.dot_general(
            weight_part, err_grad, (((1,), (1,)), ((), ())), preferred_element_type=jnp.float32
        ).astype(jnp.bfloat16),
        "tensor",
        scatter_dimension=0,
        tiled=True,
    )
    weight_part = local_weight
    down_sum = lax.dot_general(
        weight_part,
        lax.all_gather(pooled_grad_t, "seq", axis=1, tiled=True),
        (((0,), (1,)), ((), ())),
        preferred_element_type=jnp.float32,
    )
    down_grad = down_sum.astype(jnp.bfloat16).reshape(positions, groups_here, group_width)
    conv_local = jnp.einsum(
        "pkgc,pgo->gkco", windows, down_grad, preferred_element_type=jnp.float32
    )
    conv_summed = lax.psum(conv_local.astype(jnp.bfloat16), ("dp", "seq")).astype(jnp.float32)
    position_scale = 1.0 / jnp.sqrt(jnp.float32(lax.axis_size("dp") * positions * seq_count))
    conv_grad = (conv_summed * position_scale).reshape(
        groups_here, KERNEL * group_width, group_width
    )
    window_grad = jnp.einsum(
        "pgo,gkco->pkgc", down_grad, taps_weight, preferred_element_type=jnp.float32
    )
    incoming = shifted(window_grad[-1, STRIDE:], "seq", 1)
    carried_grad = jnp.concatenate([incoming[None], window_grad[:-1, STRIDE:]], axis=0)
    byte_grad = (
        (window_grad[:, :STRIDE] + carried_grad).reshape(row_total, width).astype(jnp.bfloat16)
    )
    return (downsampled[None], byte_grad[None], conv_grad, proj_grad)


def solution(mesh):
    return jax.shard_map(
        local,
        mesh=mesh,
        in_specs=(
            P("dp", "seq", "tensor"),
            P("tensor", None, None),
            P("tensor"),
            P(None, "tensor"),
            P("dp", "seq", "tensor"),
            P("dp", None),
        ),
        out_specs=(
            P("dp", "seq", "tensor"),
            P("dp", "seq", "tensor"),
            P("tensor", None, None),
            P(None, "tensor"),
        ),
        check_vma=False,
    )
```

profile of v0, /device:TPU:0, one launch (start us, length us, event | category | flops | bytes accessed | tf_op | source)
XLA Modules:
  0.0 932.5 jit_solution(48568049363792606)
XLA Ops:
  7.2 0.0 copy-start
  7.2 0.0 reduce-scatter.3.cloned.1.call-start
  7.2 0.9 slice_bitcast_fusion
  8.1 1.3 collective-permute-start
  9.4 1.0 reduce-window.9
  10.4 0.1 slice.42
  10.5 0.1 reduce-window.12
  10.5 0.1 slice_reduce_fusion
  10.6 9.0 copy.35
  19.6 10.0 %copy_dynamic-update-slice_fusion.1 = bf16[1024,8,8,128]{3,0,1,2:T(8,128)(2,1)} fusion(bf16[1024,4,8,128]{3,2,1,0:T(8,128)(2,1)} %bitcast.74), kind=kLoop, calls=%fused_computation.14 | loop fusion | bytes 16777216
  29.6 0.1 fusion.15
  29.7 9.3 fusion.5
  39.0 8.8 copy.36
  47.8 10.3 %copy_dynamic-update-slice_fusion = bf16[1024,8,8,128]{3,0,1,2:T(8,128)(2,1)} fusion(bf16[1024,8,8,128]{3,0,1,2:T(8,128)(2,1)} %copy_dynamic-update-slice_fusion.1, bf16[1024,4,8,128]{3,2,1,0:T(8,128)(2,1)} %bitcast.73), kind=kLoop, calls=%fused_computation.13 | loop fusion | bytes 16777216 | tf_op jit(solution)/shard_map/concatenate | solution.py:39
  58.1 9.1 fusion.9
  67.2 1.3 copy-done.2
  68.5 13.1 %convolution_convert_fusion.1 = bf16[4096,1024]{1,0:T(8,128)(2,1)} fusion(bf16[1024,1024]{0,1:T(8,128)(2,1)S(1)} %bitcast.78, f32[4096]{0:T(1024)S(1)} %convert_element_type.84, s32[1024]{0:T(1024)S(1)} %get-tuple-element.16, s32[4096]{0:T(1024)S(1)} %get-tuple-element.14, s32[1024]{0:T(1024)S(1)} %get-tuple-element.17, s32[4096]{0:T(1024)S(1)} %get-tuple-element.15), kind=kOutput, calls=%fused_computation.15 | convolution fusion | flops 8623489024 | bytes 10543104 | tf_op jit(solution)/shard_map/dot_general | solution.py:51
  81.6 0.0 reduce-scatter.3.cloned.1.call-update
  81.6 0.0 all-gather.3.cloned.1.call-start
  81.7 148.3 %reduce-scatter.3.cloned.1.call-done = bf16[1024,1024]{1,0:T(8,128)(2,1)} async-done(((bf16[4096,1024]{1,0:T(8,128)(2,1)}), bf16[1024,1024]{1,0:T(8,128)(2,1)}) %reduce-scatter.3.cloned.1.call-update) | async-done | bytes 2097168 | tf_op jit(solution)/shard_map/reduce_scatter | solution.py:50
  230.0 0.0 all-gather.3.cloned.1.call-update
  230.0 0.0 reduce-scatter.5.cloned.1.call-start
  230.1 59.0 %all-gather.3.cloned.1.call-done = bf16[1024,2048]{1,0:T(8,128)(2,1)} async-done(((bf16[1024,1024]{1,0:T(8,128)(2,1)}), bf16[1024,2048]{1,0:T(8,128)(2,1)}) %all-gather.3.cloned.1.call-update) | async-done | bytes 4194320 | tf_op jit(solution)/shard_map/all_gather | solution.py:56
  289.1 23.5 %fusion.16 = f32[1024,4096]{1,0:T(8,128)} fusion(bf16[1024,2048]{1,0:T(8,128)(2,1)} %all-gather.3.cloned.1.call-done, bf16[2048,4096]{1,0:T(8,128)(2,1)} %param.9), kind=kOutput, calls=%fused_computation.31 | convolution fusion | flops 17179869184 | bytes 37748736 | tf_op jit(solution)/shard_map/dot_general | solution.py:57
  312.6 28.6 %convert_bitcast_fusion = bf16[2048,1024]{0,1:T(8,128)(2,1)} fusion(bf16[2048,4096]{1,0:T(8,128)(2,1)} %param.9, f32[1024,4096]{1,0:T(8,128)} %fusion.16, bf16[1,1024,4096]{2,1,0:T(8,128)(2,1)} %param.10), kind=kOutput, calls=%fused_computation.20 | convolution fusion | flops 17194549248 | bytes 46137344 | tf_op jit(solution)/shard_map/dot_general | solution.py:67
  341.2 0.0 reduce-scatter.5.cloned.1.call-update
  341.2 0.0 all-gather.5.cloned.1.call-start
  341.3 54.4 %reduce-scatter.5.cloned.1.call-done = bf16[1024,1024]{0,1:T(8,128)(2,1)} async-done(((bf16[2048,1024]{0,1:T(8,128)(2,1)}), bf16[1024,1024]{0,1:T(8,128)(2,1)}) %reduce-scatter.5.cloned.1.call-update) | async-done | bytes 2097168 | tf_op jit(solution)/shard_map/reduce_scatter | solution.py:66
  395.7 0.0 all-gather.5.cloned.1.call-update
  395.7 11.7 %all-reduce.3.cloned.1.call-start = ((), (), s32[]{:S(2)}) async-start(), calls=%async_computation.6 | async-start | bytes 37748736 | tf_op jit(solution)/shard_map/psum | solution.py:85
  407.4 29.7 %convolution_convert_fusion = bf16[2048,4096]{1,0:T(8,128)(2,1)} fusion(bf16[1024,2048]{1,0:T(8,128)(2,1)} %all-gather.3.cloned.1.call-done, f32[1024,4096]{1,0:T(8,128)} %fusion.16, bf16[1,1024,4096]{2,1,0:T(8,128)(2,1)} %param.10), kind=kOutput, calls=%fused_computation.6 | convolution fusion | flops 17200840704 | bytes 46137344 | tf_op jit(solution)/shard_map/dot_general | solution.py:59
  437.1 109.7 %all-gather.5.cloned.1.call-done = bf16[1024,4096]{0,1:T(8,128)(2,1)} async-done(((bf16[1024,1024]{0,1:T(8,128)(2,1)}), bf16[1024,4096]{0,1:T(8,128)(2,1)}) %all-gather.5.cloned.1.call-update) | async-done | bytes 8388624 | tf_op jit(solution)/shard_map/all_gather | solution.py:77
  546.9 15.6 %fusion.12 = bf16[1024,1024]{0,1:T(8,128)(2,1)S(1)} fusion(bf16[1024,4096]{0,1:T(8,128)(2,1)} %all-gather.5.cloned.1.call-done, f32[4096]{0:T(1024)S(1)} %convert_element_type.84, s32[1024]{0:T(1024)S(1)} %get-tuple-element.16, s32[4096]{0:T(1024)S(1)} %get-tuple-element.14, s32[1024]{0:T(1024)S(1)} %get-tuple-element.17, s32[4096]{0:T(1024)S(1)} %get-tuple-element.15), kind=kOutput, calls=%fused_computation.21 | convolution fusion | flops 8620343296 | bytes 10543104 | tf_op jit(solution)/shard_map/dot_general | solution.py:75
  562.5 0.0 copy-start.1
  562.5 1.3 copy-done.1
  563.8 10.4 %convolution_convert_fusion.2 = bf16[8,8,128,128]{3,2,1,0:T(8,128)(2,1)} fusion(bf16[1024,8,8,128]{3,0,1,2:T(8,128)(2,1)} %copy_dynamic-update-slice_fusion, bf16[1024,8,128,1]{0,2,3,1:T(8,128)(2,1)S(1)} %bitcast.75), kind=kOutput, calls=%fused_computation.22 | convolution fusion | flops 2148532224 | bytes 20971520 | tf_op jit(solution)/shard_map/pkgc,pgo->gkco/dot_general | solution.py:82
  574.2 0.0 all-reduce.3.cloned.1.call-update
  574.2 15.7 %convolution_bitcast_fusion = f32[1024,8,8,128]{3,0,1,2:T(8,128)} fusion(bf16[1024,8,128,1]{0,2,3,1:T(8,128)(2,1)} %bitcast.76, bf16[8,8,128,128]{3,2,1,0:T(8,128)(2,1)S(1)} %bitcast.70), kind=kOutput, calls=%fused_computation.7 | convolution fusion | flops 2147483648 | bytes 37748736 | tf_op jit(solution)/shard_map/pgo,gkco->pkgc/dot_general | solution.py:90
  589.9 0.9 slice.45
  590.8 1.3 collective-permute-start.1
  592.1 4.0 copy.24
  596.1 6.8 slice.46
  602.9 9.7 %fusion = bf16[1024,4,8,128]{3,0,1,2:T(8,128)(2,1)} fusion(f32[1024,8,8,128]{3,0,1,2:T(8,128)} %convolution_bitcast_fusion, f32[1023,4,8,128]{3,0,1,2:T(8,128)S(1)} %slice.46, f32[1,4,8,128]{3,0,1,2:T(1,128)S(1)} %bitcast.83), kind=kLoop, calls=%fused_computation.2 | loop fusion | flops 12582912 | bytes 41943040 | tf_op jit(solution)/shard_map/convert_element_type | solution.py:96
  612.6 12.3 %copy.21 = bf16[1024,4,8,128]{3,2,1,0:T(8,128)(2,1)} copy(bf16[1024,4,8,128]{3,0,1,2:T(8,128)(2,1)} %fusion) | data formatting | bytes 16777216 | tf_op jit(solution)/shard_map/convert_element_type | solution.py:96
  624.9 13.6 %convert_element_type.95 = bf16[1,4096,1024]{2,1,0:T(8,128)(2,1)} reshape(bf16[1024,4,8,128]{3,2,1,0:T(8,128)(2,1)} %copy.21) | data formatting | bytes 16777216 | tf_op jit(solution)/shard_map/convert_element_type | solution.py:96
  638.4 264.3 %all-reduce.3.cloned.1.call-done = (bf16[8,8,128,128]{3,2,1,0:T(8,128)(2,1)}, bf16[2048,4096]{1,0:T(8,128)(2,1)}) async-done(((bf16[8,8,128,128]{3,2,1,0:T(8,128)(2,1)}, bf16[2048,4096]{1,0:T(8,128)(2,1)}), (bf16[8,8,128,128]{3,2,1,0:T(8,128)(2,1)}, bf16[2048,4096]{1,0:T(8,128)(2,1)})) %all-reduce.3.cloned.1.call-update) | async-done | bytes 18874384 | tf_op jit(solution)/shard_map/psum | solution.py:85
  902.8 4.2 convert_multiply_fusion.1
  906.9 18.7 %convert_multiply_fusion = f32[2048,4096]{1,0:T(8,128)} fusion(bf16[2048,4096]{1,0:T(8,128)(2,1)} %get-tuple-element.13), kind=kLoop, calls=%fused_computation | loop fusion | flops 16777216 | bytes 50331648 | tf_op jit(solution)/shard_map/mul | solution.py:64
  (10 shorter events, 0.0 us)
Async XLA Ops:
  7.2 50.9 %copy-start = (bf16[8,1024,128]{2,1,0:T(8,128)(2,1)S(1)}, bf16[8,1024,128]{2,1,0:T(8,128)(2,1)}, u32[]{:S(2)}) copy-start(bf16[8,1024,128]{2,1,0:T(8,128)(2,1)} %param.7) | copy-start | bytes 6291460
  7.2 222.8 %reduce-scatter.3.cloned.1.call-start = ((), (), s32[]{:S(2)}) async-start(), calls=%async_computation.2 | async-start | bytes 10485760 | tf_op jit(solution)/shard_map/reduce_scatter | solution.py:50
  8.1 21.6 %collective-permute-start = (bf16[4,1024]{1,0:T(4,128)(2,1)S(1)}, bf16[4,1024]{1,0:T(4,128)(2,1)S(1)}, u32[]{:S(2)}, u32[]{:S(2)}) collective-permute-start(bf16[4,1024]{1,0:T(4,128)(2,1)S(1)} %slice_bitcast_fusion), channel_id=1, source_target_pairs={{2,0},{4,2},{6,4},{3,1},{5,3},{7,5},{10,8},{12,10},{14,12},{11,9},... | collective-permute-start | bytes 24584 | tf_op jit(solution)/shard_map/ppermute | solution.py:13
  19.6 10.0 %copy-start.3 = (s32[1,4096]{1,0:T(1,128)S(1)}, s32[1,4096]{1,0:T(1,128)}, u32[]{:S(2)}) copy-start(s32[1,4096]{1,0:T(1,128)} %param.11) | copy-start | bytes 49156
  47.8 10.3 %copy-start.4 = (f32[1024]{0:T(1024)S(1)}, f32[1024]{0:T(1024)}, u32[]{:S(2)}) copy-start(f32[1024]{0:T(1024)} %param.8) | copy-start | bytes 12292
  67.2 1.3 copy-start.2
  81.6 207.4 %all-gather.3.cloned.1.call-start = ((), (), s32[]{:S(2)}) async-start(), calls=%async_computation.3 | async-start | bytes 6291456 | tf_op jit(solution)/shard_map/all_gather | solution.py:56
  230.0 165.6 %reduce-scatter.5.cloned.1.call-start = ((), (), s32[]{:S(2)}) async-start(), calls=%async_computation.4 | async-start | bytes 6291456 | tf_op jit(solution)/shard_map/reduce_scatter | solution.py:66
  341.2 205.6 %all-gather.5.cloned.1.call-start = ((), (), s32[]{:S(2)}) async-start(), calls=%async_computation.5 | async-start | bytes 10485760 | tf_op jit(solution)/shard_map/all_gather | solution.py:77
  395.7 507.1 %all-reduce.3.cloned.1.call-start = ((), (), s32[]{:S(2)}) async-start(), calls=%async_computation.6 | async-start | bytes 37748736 | tf_op jit(solution)/shard_map/psum | solution.py:85
  562.5 1.3 copy-start.1
  590.8 12.1 %collective-permute-start.1 = (f32[4,8,128]{2,0,1:T(4,128)S(1)}, f32[4,8,128]{2,0,1:T(4,128)S(1)}, u32[]{:S(2)}, u32[]{:S(2)}) collective-permute-start(f32[4,8,128]{2,0,1:T(4,128)S(1)} %bitcast.84), channel_id=1, source_target_pairs={{0,2},{2,4},{4,6},{1,3},{3,5},{5,7},{8,10},{10,12},{12,14},{9,11},... | collective-permute-start | bytes 49160 | tf_op jit(solution)/shard_map/ppermute | solution.py:13
Sparse Core Ops, SparseCore 0:
  81.8 148.2 reduce-scatter.2
  231.6 57.4 all-gather.2
  341.4 54.2 reduce-scatter.4
  397.2 149.6 all-gather.4
  574.3 328.3 all-reduce.2
where the time goes:
time: 942 us; the launch traced here: 933 us
  waiting for transfers between devices  636 us (68%)
  matrix products  146 us (15%)
  local copies, waits for them, and re-layouts  79.3 us (8%)
  other arithmetic  42.9 us (5%)
  starting transfers between devices  14.4 us (2%)
  between operations  14.3 us (2%)
    psum x1, waiting for transfers between devices, local(): lax.psum(conv_local.astype(jnp.bfloat16), ('dp', 'seq')).astype(jnp.float32)  264 us
    reduce_scatter x1, waiting for transfers between devices, local(): lax.psum_scatter(jnp.dot(weight_part, downsampled, preferred_element_type...  148 us
    all_gather x1, waiting for transfers between devices, local(): lax.all_gather(pooled_grad_t, 'seq', axis=1, tiled=True)  110 us
    all_gather x1, waiting for transfers between devices, local(): gathered = lax.all_gather(pooled_sum, 'tensor', axis=1, tiled=True)  59 us
    reduce_scatter x1, waiting for transfers between devices, local(): lax.psum_scatter(lax.dot_general(weight_part, err_grad, (((1,), (1,)), ((...  54.4 us
    unnamed x14, local copies, waits for them, and re-layouts  34.4 us
    dot_general x1, matrix products, local(): lax.dot_general(gathered, err_grad, (((0,), (0,)), ((), ())), preferred_e...  29.7 us
    dot_general x1, matrix products, local(): lax.dot_general(weight_part, err_grad, (((1,), (1,)), ((), ())), preferre...  28.6 us
  transfers between devices with their start and end apart: 7, of which 5 were waited for; matrix products, arithmetic and copies ran while one was open for 12% of the time, Pallas kernels for 0%

commit v1 on v0

v1 whole, which is shorter than its diff:
```python
import jax
import jax.numpy as jnp
from jax import lax
from jax.sharding import PartitionSpec as P

STRIDE = 4
KERNEL = 8
FORWARD_CHUNKS = 2
BACKWARD_CHUNKS = 2
PROJ_CHUNKS = 2
F32 = jnp.float32
BF16 = jnp.bfloat16


def shifted(block, axis, distance):
    devices = range(lax.axis_size(axis))
    route = [(i - distance, i) for i in devices if i - distance in devices]
    return lax.ppermute(block, axis, route)


def ring(block, axis):
    count = lax.axis_size(axis)
    return lax.ppermute(block, axis, [(i, (i + 1) % count) for i in range(count)])


def swapped(block, axis, bit):
    count = lax.axis_size(axis)
    return lax.ppermute(block, axis, [(i, i ^ bit) for i in range(count)])


def prefix_sum(lengths):
    total = lengths.shape[0]
    cols = 128
    rows = total // cols
    table = lengths.reshape(rows, cols)
    col = jnp.arange(cols, dtype=jnp.int32)
    row = jnp.arange(rows, dtype=jnp.int32)
    inside = jnp.sum(
        jnp.where(col[None, :, None] >= col[None, None, :], table[:, None, :], 0), axis=2
    )
    row_total = jnp.sum(table, axis=1)
    before = jnp.sum(jnp.where(row[:, None] > row[None, :], row_total[None, :], 0), axis=1)
    return (inside + before[:, None]).reshape(total)


def intersection_weights(span_start, span_end, span_lengths, first_position, position_count):
    byte_first = (first_position + jnp.arange(position_count, dtype=jnp.int32)) * STRIDE
    lower_edge = jnp.maximum(span_start[:, None], byte_first[None, :])
    upper_edge = jnp.minimum(span_end[:, None], byte_first[None, :] + STRIDE)
    covered = jnp.maximum(upper_edge - lower_edge, 0).astype(F32)
    return (covered / span_lengths[:, None].astype(F32)).astype(BF16)


def halves(block, own):
    half = block.shape[0] // 2
    mine = lax.dynamic_slice_in_dim(block, own * half, half, 0)
    other = lax.dynamic_slice_in_dim(block, (1 - own) * half, half, 0)
    return mine, other


def rejoined(mine, other, own):
    return jnp.where(
        own == 0,
        jnp.concatenate([mine, other], axis=0),
        jnp.concatenate([other, mine], axis=0),
    )


def added(a, b):
    return (a.astype(F32) + b.astype(F32)).astype(BF16)


def summed_product(rows_t, right):
    dp_count = lax.axis_size("dp")
    dp_rank = lax.axis_index("dp")
    seq_count = lax.axis_size("seq")
    seq_rank = lax.axis_index("seq")
    bits = [1 << i for i in range(dp_count.bit_length() - 1)]

    def product(columns):
        return lax.dot_general(
            columns, right, (((0,), (0,)), ((), ())), preferred_element_type=F32
        )

    half = rows_t.shape[1] // 2
    own = dp_rank % 2
    send = product(lax.dynamic_slice_in_dim(rows_t, (1 - own) * half, half, 1)).astype(BF16)
    got = swapped(send, "dp", 1)
    mine = product(lax.dynamic_slice_in_dim(rows_t, own * half, half, 1))
    held = (mine + got.astype(F32)).astype(BF16)
    for bit in bits[1:]:
        keep, give = halves(held, dp_rank // bit % 2)
        held = added(keep, swapped(give, "dp", bit))
    depth = held.shape[0] // seq_count

    def part(index):
        return lax.dynamic_slice_in_dim(held, (index + seq_count) % seq_count * depth, depth, 0)

    moving = part(seq_rank - 1)
    for step in range(seq_count - 1):
        moving = added(ring(moving, "seq"), part(seq_rank - 2 - step))
    held = lax.all_gather(moving, "seq", axis=0, tiled=True)
    for bit in bits[::-1]:
        held = rejoined(held, swapped(held, "dp", bit), dp_rank // bit % 2)
    return held


def local(byte_acts, conv_weight, conv_bias, proj_weight, teacher, span_lengths):
    byte_rows = byte_acts[0]
    row_total, width = byte_rows.shape
    groups_here = conv_weight.shape[0]
    group_width = width // groups_here
    positions = row_total // STRIDE
    seq_count = lax.axis_size("seq")
    seq_rank = lax.axis_index("seq")
    dp_count = lax.axis_size("dp")
    tensor_count = lax.axis_size("tensor")
    tensor_rank = lax.axis_index("tensor")
    lengths_doc = span_lengths[0]
    tokens_all = lengths_doc.shape[0]
    tokens = tokens_all // seq_count
    span_end = prefix_sum(lengths_doc)
    span_start = span_end - lengths_doc

    def own_tokens(values):
        return lax.dynamic_slice_in_dim(values, seq_rank * tokens, tokens, 0)

    token_weight = intersection_weights(
        own_tokens(span_start),
        own_tokens(span_end),
        own_tokens(lengths_doc),
        0,
        positions * seq_count,
    )
    local_weight = intersection_weights(
        span_start, span_end, lengths_doc, seq_rank * positions, positions
    )

    next_rows = shifted(byte_rows[:STRIDE], "seq", -1)
    blocks = byte_rows.reshape(positions, STRIDE, groups_here, group_width)
    halo = next_rows.reshape(STRIDE, groups_here, group_width)
    taps = conv_weight.reshape(groups_here, 2, STRIDE, group_width, group_width)
    taps_pair = jnp.transpose(taps, (0, 2, 3, 1, 4)).reshape(
        groups_here, STRIDE, group_width, 2 * group_width
    )
    forward_chunks = min(FORWARD_CHUNKS, groups_here)
    backward_chunks = min(BACKWARD_CHUNKS, groups_here)

    per = groups_here // forward_chunks
    down_parts = []
    gathered_parts = []
    for chunk in range(forward_chunks):
        sel = slice(chunk * per, (chunk + 1) * per)
        both = jnp.einsum(
            "pkgc,gkcn->pgn", blocks[:, :, sel], taps_pair[sel], preferred_element_type=F32
        )
        tail = jnp.einsum(
            "kgc,gkco->go", halo[:, sel], taps[sel, 1], preferred_element_type=F32
        )
        later = jnp.concatenate([both[1:, :, group_width:], tail[None]], axis=0)
        bias = conv_bias.reshape(groups_here, group_width)[sel]
        part = both[:, :, :group_width] + later + bias[None]
        part = part.reshape(positions, per * group_width).astype(BF16)
        down_parts.append(part)
        whole = lax.all_gather(part, "seq", axis=0, tiled=True)
        pooled = jnp.dot(token_weight, whole, preferred_element_type=F32).astype(BF16)
        gathered_parts.append(lax.all_gather(pooled, "tensor", axis=1, tiled=False))
    downsampled = jnp.concatenate(down_parts, axis=1)
    gathered = jnp.concatenate(gathered_parts, axis=2).reshape(tokens, tensor_count * width)

    predicted = jnp.dot(gathered, proj_weight, preferred_element_type=F32)
    err_grad = (predicted - teacher[0].astype(F32)).astype(BF16)

    weight_blocks = proj_weight.reshape(tensor_count, width, proj_weight.shape[1])
    per = groups_here // backward_chunks
    span = per * group_width
    token_grads = []
    for chunk in range(backward_chunks):
        weight_part = weight_blocks[:, chunk * span : (chunk + 1) * span]
        if tensor_count == 2:
            def back(block):
                return lax.dot_general(
                    lax.dynamic_index_in_dim(weight_part, block, 0, keepdims=False),
                    err_grad,
                    (((1,), (1,)), ((), ())),
                    preferred_element_type=F32,
                ).astype(BF16)

            got = swapped(back(1 - tensor_rank), "tensor", 1)
            pooled_grad_t = added(back(tensor_rank), got)
        else:
            pooled_grad_t = lax.psum_scatter(
                lax.dot_general(
                    weight_part.reshape(tensor_count * span, -1),
                    err_grad,
                    (((1,), (1,)), ((), ())),
                    preferred_element_type=F32,
                ).astype(BF16),
                "tensor",
                scatter_dimension=0,
                tiled=True,
            )
        token_grads.append(lax.all_gather(pooled_grad_t, "seq", axis=1, tiled=True))

    chunk_rows = gathered.shape[1] // PROJ_CHUNKS
    token_scale = 1.0 / jnp.sqrt(F32(dp_count * tokens_all))
    proj_parts = [
        summed_product(gathered[:, i * chunk_rows : (i + 1) * chunk_rows], err_grad)
        for i in range(PROJ_CHUNKS)
    ]

    position_scale = 1.0 / jnp.sqrt(F32(dp_count * positions * seq_count))
    byte_parts = []
    conv_parts = []
    for chunk in range(backward_chunks):
        sel = slice(chunk * per, (chunk + 1) * per)
        down = lax.dot_general(
            local_weight,
            token_grads[chunk],
            (((0,), (1,)), ((), ())),
            preferred_element_type=F32,
        ).astype(BF16)
        before = shifted(down[-1:], "seq", 1)
        earlier = jnp.concatenate([before, down[:-1]], axis=0)
        pair = jnp.concatenate(
            [
                down.reshape(positions, per, group_width),
                earlier.reshape(positions, per, group_width),
            ],
            axis=2,
        )
        grads = jnp.einsum(
            "pkgc,pgn->gkcn", blocks[:, :, sel], pair, preferred_element_type=F32
        )
        grads = grads.reshape(per, STRIDE, group_width, 2, group_width)
        conv_parts.append(jnp.transpose(grads, (0, 3, 1, 2, 4)))
        part = jnp.einsum(
            "pgn,gkcn->pkgc", pair, taps_pair[sel], preferred_element_type=F32
        )
        byte_parts.append(part.astype(BF16))
    byte_grad = jnp.concatenate(byte_parts, axis=2).reshape(row_total, width)
    conv_local = jnp.concatenate(conv_parts, axis=0)
    conv_summed = lax.psum(conv_local.astype(BF16), ("dp", "seq")).astype(F32)
    conv_grad = (conv_summed * position_scale).reshape(
        groups_here, KERNEL * group_width, group_width
    )
    proj_grad = jnp.concatenate([p.astype(F32) * token_scale for p in proj_parts], axis=0)
    return (downsampled[None], byte_grad[None], conv_grad, proj_grad)


def solution(mesh):
    return jax.shard_map(
        local,
        mesh=mesh,
        in_specs=(
            P("dp", "seq", "tensor"),
            P("tensor", None, None),
            P("tensor"),
            P(None, "tensor"),
            P("dp", "seq", "tensor"),
            P("dp", None),
        ),
        out_specs=(
            P("dp", "seq", "tensor"),
            P("dp", "seq", "tensor"),
            P("tensor", None, None),
            P(None, "tensor"),
        ),
        check_vma=False,
    )
```

time: 942 us -> 882 us (0.936)
  waiting for transfers between devices: 636 us -> 503 us
  other arithmetic: 42.9 us -> 76 us
  starting transfers between devices: 14.4 us -> 42.3 us
  local copies, waits for them, and re-layouts: 79.3 us -> 93 us
    psum x1, waiting for transfers between devices: 264 us -> 57.9 us  [local(): conv_summed = lax.psum(conv_local.astype(BF16), ('dp', 'seq')).astype(F32)]
    reduce_scatter x2 -> x0, waiting for transfers between devices: 203 us -> none  [the longest x1 148 us: local(): lax.psum_scatter(jnp.dot(weight_part, downsampled, preferred_element_type...]
    ppermute x0 -> x16, waiting for transfers between devices: none -> 173 us  [the longest x6 106 us: ring(): lax.ppermute(block, axis, [(i, (i + 1) % count) for i in range(count)])]
    all_gather x2 -> x8, waiting for transfers between devices: 169 us -> 271 us  [the longest x2 148 us: local(): whole = lax.all_gather(part, 'seq', axis=0, tiled=True)]
    ppermute x0 -> x16, starting transfers between devices: none -> 34.3 us  [the longest x6 26.9 us: ring(): lax.ppermute(block, axis, [(i, (i + 1) % count) for i in range(count)])]
    concatenate x0 -> x4, other arithmetic: none -> 28.3 us  [the longest x1 11.7 us: local(): jnp.concatenate([p.astype(F32) * token_scale for p in proj_parts], axis=0)]
    convert_element_type x2, local copies, waits for them, and re-layouts: 25.9 us -> 1.09 us  [local(): part = part.reshape(positions, per * group_width).astype(BF16)]
    slice x3 -> x10, local copies, waits for them, and re-layouts: 7.83 us -> 23.2 us  [the longest x1 10.2 us: local(): blocks[:, :, sel]]
  transfers between devices with their start and end apart: 7 -> 28, of which waited for: 5 -> 17; matrix products, arithmetic and copies ran while one was open for 12% -> 26% of each run, Pallas kernels for 0% -> 0%
where the time goes in v1:
time: 882 us; the launch traced here: 874 us
  waiting for transfers between devices  503 us (57%)
  matrix products  145 us (16%)
  local copies, waits for them, and re-layouts  93 us (11%)
  other arithmetic  76 us (9%)
  starting transfers between devices  42.3 us (5%)
  between operations  14.7 us (2%)
    all_gather x2, waiting for transfers between devices, local(): whole = lax.all_gather(part, 'seq', axis=0, tiled=True)  148 us
    ppermute x6, waiting for transfers between devices, ring(): lax.ppermute(block, axis, [(i, (i + 1) % count) for i in range(count)])  106 us
    ppermute x10, waiting for transfers between devices, swapped(): return lax.ppermute(block, axis, [(i, i ^ bit) for i in range(count)])  67.7 us
    all_gather x2, waiting for transfers between devices, local(): token_grads.append(lax.all_gather(pooled_grad_t, 'seq', axis=1, tiled=True))  65.9 us
    psum x1, waiting for transfers between devices, local(): conv_summed = lax.psum(conv_local.astype(BF16), ('dp', 'seq')).astype(F32)  57.9 us
    all_gather x2, waiting for transfers between devices, local(): gathered_parts.append(lax.all_gather(pooled, 'tensor', axis=1, tiled=False))  56.5 us
    dot_general x4, matrix products, back(): lax.dot_general(lax.dynamic_index_in_dim(weight_part, block, 0, keepdims=...  35.3 us
    dot_general x4, matrix products, product(): lax.dot_general(columns, right, (((0,), (0,)), ((), ())), preferred_eleme...  32.9 us
  transfers between devices with their start and end apart: 28, of which 17 were waited for; matrix products, arithmetic and copies ran while one was open for 26% of the time, Pallas kernels for 0%

profile of v1, /device:TPU:0, one launch (start us, length us, event | category | flops | bytes accessed | tf_op | source)
XLA Modules:
  0.0 873.6 jit_solution(3817302297335135309)
XLA Ops:
  12.5 9.7 %copy.78 = bf16[512,8,8,128]{3,2,1,0:T(8,128)(2,1)} copy(bf16[512,8,8,128]{3,1,2,0:T(8,128)(2,1)} %bitcast.176) | data formatting | bytes 16777216
  22.2 10.2 %fusion.92 = (bf16[1024,4,4,128]{3,2,1,0:T(4,128)(2,1)}, bf16[1024,4,4,128]{3,2,1,0:T(4,128)(2,1)S(1)}) fusion(bf16[1024,4,8,128]{3,2,1,0:T(8,128)(2,1)} %bitcast.167), kind=kLoop, calls=%fused_computation.133 | loop fusion | bytes 16777216 | tf_op jit(solution)/shard_map/slice | solution.py:155
  46.2 76.4 %all-gather.13.cloned.1.call-done = bf16[4096,512]{0,1:T(8,128)(2,1)} async-done(((bf16[1024,512]{0,1:T(8,128)(2,1)}), bf16[4096,512]{0,1:T(8,128)(2,1)}) %all-gather.13.cloned.1.call-update) | async-done | bytes 4194320 | tf_op jit(solution)/shard_map/all_gather | solution.py:165
  122.5 8.8 %fusion.50 = bf16[1024,512]{1,0:T(8,128)(2,1)} fusion(bf16[4096,512]{0,1:T(8,128)(2,1)} %all-gather.13.cloned.1.call-done, f32[1024]{0:T(1024)S(1)} %bitcast.196, s32[4096]{0:T(1024)S(1)} %get-tuple-element.20, s32[1024]{0:T(1024)S(1)} %dynamic_slice.72, s32[4096]{0:T(1024)S(1)} %get-tuple-element.21, s32[1024]{0:T(1024)S(1)} %dynamic_slice.71), kind=kOutput, calls=%fused_computation.68 | convolution fusion | flops 4324851712 | bytes 5287936 | tf_op jit(solution)/shard_map/dot_general | solution.py:166
  131.6 71.8 %all-gather.11.cloned.1.call-done = bf16[4096,512]{0,1:T(8,128)(2,1)} async-done(((bf16[1024,512]{0,1:T(8,128)(2,1)}), bf16[4096,512]{0,1:T(8,128)(2,1)}) %all-gather.11.cloned.1.call-update) | async-done | bytes 4194320 | tf_op jit(solution)/shard_map/all_gather | solution.py:165
  203.4 8.8 %fusion.49 = bf16[1024,512]{1,0:T(8,128)(2,1)} fusion(bf16[4096,512]{0,1:T(8,128)(2,1)} %all-gather.11.cloned.1.call-done, f32[1024]{0:T(1024)S(1)} %bitcast.197, s32[4096]{0:T(1024)S(1)} %get-tuple-element.20, s32[1024]{0:T(1024)S(1)} %dynamic_slice.72, s32[4096]{0:T(1024)S(1)} %get-tuple-element.21, s32[1024]{0:T(1024)S(1)} %dynamic_slice.71), kind=kOutput, calls=%fused_computation.67 | convolution fusion | flops 4324851712 | bytes 5287936 | tf_op jit(solution)/shard_map/dot_general | solution.py:166
  212.5 24.7 %all-gather.25.cloned.1.call-done = bf16[1024,1024]{1,0:T(8,128)(2,1)} async-done(((bf16[1024,512]{1,0:T(8,128)(2,1)}), bf16[1024,1024]{1,0:T(8,128)(2,1)}) %all-gather.25.cloned.1.call-update) | async-done | bytes 2097168 | tf_op jit(solution)/shard_map/all_gather | solution.py:167
  240.6 31.8 %all-gather.23.cloned.1.call-done = bf16[1024,1024]{1,0:T(8,128)(2,1)} async-done(((bf16[1024,512]{1,0:T(8,128)(2,1)}), bf16[1024,1024]{1,0:T(8,128)(2,1)}) %all-gather.23.cloned.1.call-update) | async-done | bytes 2097168 | tf_op jit(solution)/shard_map/all_gather | solution.py:167
  272.4 4.5 reshape.169
  276.8 7.4 pad_maximum_fusion.2
  289.6 25.0 %fusion = bf16[1024,4096]{1,0:T(8,128)(2,1)} fusion(bf16[1024,2048]{1,0:T(8,128)(2,1)S(1)} %bitcast.170, bf16[2048,4096]{1,0:T(8,128)(2,1)} %param.9, bf16[1,1024,4096]{2,1,0:T(8,128)(2,1)} %param.10), kind=kOutput, calls=%fused_computation.2 | convolution fusion | flops 17192452096 | bytes 37748736 | tf_op jit(solution)/shard_map/dot_general | solution.py:171
  314.6 10.3 %convolution_convert_fusion = bf16[512,4096]{1,0:T(8,128)(2,1)} fusion(bf16[1024,4096]{1,0:T(8,128)(2,1)} %fusion, bf16[1024,1024]{1,0:T(8,128)(2,1)} %get-tuple-element.11, s32[]{:T(128)S(6)} %select_n.145), kind=kOutput, calls=%fused_computation.16 | convolution fusion | flops 4297064448 | bytes 13631492 | tf_op jit(solution)/shard_map/dot_general | solution.py:81
  324.9 9.8 %fusion.91 = (bf16[2,512,4096]{2,1,0:T(8,128)(2,1)}, bf16[2,512,4096]{2,1,0:T(8,128)(2,1)S(1)}) fusion(bf16[2,1024,4096]{2,1,0:T(8,128)(2,1)} %bitcast.168), kind=kLoop, calls=%fused_computation.132 | loop fusion | bytes 33554432 | tf_op jit(solution)/shard_map/slice | solution.py:179
  337.3 5.5 fusion.44
  343.1 6.4 convolution_convert_fusion.1
  349.7 6.7 add_convert_fusion
  360.4 8.3 collective-permute-done.3
  368.7 10.3 %add_convert_fusion.4 = bf16[512,1024]{1,0:T(8,128)(2,1)} fusion(bf16[512,1024]{1,0:T(8,128)(2,1)} %collective-permute-done.3, bf16[1024,4096]{1,0:T(8,128)(2,1)} %fusion, bf16[2,512,4096]{2,1,0:T(8,128)(2,1)} %copy-done.9, s32[]{:T(128)S(6)} %select_n.136), kind=kOutput, calls=%fused_computation.58 | convolution fusion | flops 4297588736 | bytes 14680068 | tf_op jit(solution)/shard_map/dot_general | solution.py:182
  379.1 27.5 %collective-permute-done.13 = bf16[256,4096]{1,0:T(8,128)(2,1)} collective-permute-done((bf16[256,4096]{1,0:T(8,128)(2,1)S(1)}, bf16[256,4096]{1,0:T(8,128)(2,1)}, u32[]{:S(2)}, u32[]{:S(2)}) %collective-permute-start.13) | collective-permute-done | bytes 2097184 | tf_op jit(solution)/shard_map/ppermute | solution.py:28
  411.5 9.5 %add_convert_fusion.1 = bf16[512,4096]{1,0:T(8,128)(2,1)S(1)} fusion(bf16[512,4096]{1,0:T(8,128)(2,1)} %collective-permute-done.5, bf16[1024,4096]{1,0:T(8,128)(2,1)} %fusion, bf16[1024,1024]{1,0:T(8,128)(2,1)} %copy-done.11, s32[]{:T(128)S(6)} %select_n.144), kind=kOutput, calls=%fused_computation.11 | convolution fusion | flops 4301258752 | bytes 17825796 | tf_op jit(solution)/shard_map/dot_general | solution.py:81
  426.1 11.0 %collective-permute-done.14 = bf16[64,4096]{1,0:T(8,128)(2,1)S(1)} collective-permute-done((bf16[64,4096]{1,0:T(8,128)(2,1)S(1)}, bf16[64,4096]{1,0:T(8,128)(2,1)S(1)}, u32[]{:S(2)}, u32[]{:S(2)}) %collective-permute-start.14) | collective-permute-done | bytes 524320 | tf_op jit(solution)/shard_map/ppermute | solution.py:23
  437.2 9.0 %collective-permute-start.15 = (bf16[64,4096]{1,0:T(8,128)(2,1)S(1)}, bf16[64,4096]{1,0:T(8,128)(2,1)S(1)}, u32[]{:S(2)}, u32[]{:S(2)}) collective-permute-start(bf16[64,4096]{1,0:T(8,128)(2,1)S(1)} %add_convert_fusion.8), channel_id=1, source_target_pairs={{0,2},{2,4},{4,6},{6,0},{1,3},{3,5},{5,7},{7,1},{8,10},{10,12},{12... | collective-permute-start | bytes 1572872 | tf_op jit(solution)/shard_map/ppermute | solution.py:23
  446.2 27.4 %collective-permute-done.15 = bf16[64,4096]{1,0:T(8,128)(2,1)S(1)} collective-permute-done((bf16[64,4096]{1,0:T(8,128)(2,1)S(1)}, bf16[64,4096]{1,0:T(8,128)(2,1)S(1)}, u32[]{:S(2)}, u32[]{:S(2)}) %collective-permute-start.15) | collective-permute-done | bytes 524320 | tf_op jit(solution)/shard_map/ppermute | solution.py:23
  473.7 6.0 collective-permute-start.16
  486.6 8.8 %collective-permute-done.16 = bf16[64,4096]{1,0:T(8,128)(2,1)S(1)} collective-permute-done((bf16[64,4096]{1,0:T(8,128)(2,1)S(1)}, bf16[64,4096]{1,0:T(8,128)(2,1)S(1)}, u32[]{:S(2)}, u32[]{:S(2)}) %collective-permute-start.16) | collective-permute-done | bytes 524320 | tf_op jit(solution)/shard_map/ppermute | solution.py:23
  496.4 9.4 %collective-permute-done.7 = bf16[64,4096]{1,0:T(8,128)(2,1)S(1)} collective-permute-done((bf16[64,4096]{1,0:T(8,128)(2,1)S(1)}, bf16[64,4096]{1,0:T(8,128)(2,1)S(1)}, u32[]{:S(2)}, u32[]{:S(2)}) %collective-permute-start.7) | collective-permute-done | bytes 524320 | tf_op jit(solution)/shard_map/ppermute | solution.py:23
  507.0 27.2 %collective-permute-done.8 = bf16[64,4096]{1,0:T(8,128)(2,1)S(1)} collective-permute-done((bf16[64,4096]{1,0:T(8,128)(2,1)S(1)}, bf16[64,4096]{1,0:T(8,128)(2,1)S(1)}, u32[]{:S(2)}, u32[]{:S(2)}) %collective-permute-start.8) | collective-permute-done | bytes 524320 | tf_op jit(solution)/shard_map/ppermute | solution.py:23
  535.4 7.5 collective-permute-start.9
  542.9 21.7 %collective-permute-done.9 = bf16[64,4096]{1,0:T(8,128)(2,1)S(1)} collective-permute-done((bf16[64,4096]{1,0:T(8,128)(2,1)S(1)}, bf16[64,4096]{1,0:T(8,128)(2,1)S(1)}, u32[]{:S(2)}, u32[]{:S(2)}) %collective-permute-start.9) | collective-permute-done | bytes 524320 | tf_op jit(solution)/shard_map/ppermute | solution.py:23
  566.8 9.2 %fusion.38 = bf16[512,1024]{1,0:T(8,128)(2,1)S(1)} fusion(bf16[1024,4096]{1,0:T(8,128)(2,1)} %fusion, bf16[2,512,4096]{2,1,0:T(8,128)(2,1)} %get-tuple-element.6, s32[]{:T(128)S(6)} %select_n.138), kind=kOutput, calls=%fused_computation.62 | convolution fusion | flops 4295491584 | bytes 13631492 | tf_op jit(solution)/shard_map/dot_general | solution.py:182
  577.6 22.6 %collective-permute-done.1 = bf16[512,1024]{1,0:T(8,128)(2,1)S(1)} collective-permute-done((bf16[512,1024]{1,0:T(8,128)(2,1)S(1)}, bf16[512,1024]{1,0:T(8,128)(2,1)S(1)}, u32[]{:S(2)}, u32[]{:S(2)}) %collective-permute-start.1) | collective-permute-done | bytes 1048608 | tf_op jit(solution)/shard_map/ppermute | solution.py:28
  600.2 10.2 %add_convert_fusion.5 = bf16[512,1024]{1,0:T(8,128)(2,1)} fusion(bf16[512,1024]{1,0:T(8,128)(2,1)S(1)} %collective-permute-done.1, bf16[1024,4096]{1,0:T(8,128)(2,1)} %fusion, bf16[2,512,4096]{2,1,0:T(8,128)(2,1)} %get-tuple-element.6, s32[]{:T(128)S(6)} %select_n.136), kind=kOutput, calls=%fused_computation.59 | convolution fusion | flops 4297588736 | bytes 14680068 | tf_op jit(solution)/shard_map/dot_general | solution.py:182
  613.5 8.5 fusion.48
  626.0 65.9 %all-gather.15.cloned.1.call-done = bf16[512,4096]{1,0:T(8,128)(2,1)} async-done(((bf16[512,1024]{1,0:T(8,128)(2,1)}), bf16[512,4096]{1,0:T(8,128)(2,1)}) %all-gather.15.cloned.1.call-update) | async-done | bytes 4194320 | tf_op jit(solution)/shard_map/all_gather | solution.py:203
  691.9 8.5 fusion.47
  700.4 4.9 maximum_select_fusion.3
  705.5 9.3 %collective-permute-done.10 = bf16[256,4096]{1,0:T(8,128)(2,1)} collective-permute-done((bf16[256,4096]{1,0:T(8,128)(2,1)}, bf16[256,4096]{1,0:T(8,128)(2,1)}, u32[]{:S(2)}, u32[]{:S(2)}) %collective-permute-start.10) | collective-permute-done | bytes 2097184 | tf_op jit(solution)/shard_map/ppermute | solution.py:28
  714.8 4.8 maximum_select_fusion.2
  729.9 4.6 convert_bitcast_fusion
  737.8 7.6 pad_maximum_fusion.1
  745.4 12.4 %copy.52 = bf16[1024,4,8,128]{3,2,1,0:T(8,128)(2,1)} copy(bf16[1024,4,8,128]{3,0,1,2:T(8,128)(2,1)} %pad_maximum_fusion.1) | data formatting | bytes 16777216 | tf_op jit(solution)/shard_map/concatenate | solution.py:241
  757.9 13.4 %broadcast_in_dim_reshape.4 = bf16[1,4096,1024]{2,1,0:T(8,128)(2,1)} reshape(bf16[1024,4,8,128]{3,2,1,0:T(8,128)(2,1)} %copy.52) | data formatting | bytes 16777216 | tf_op jit(solution)/shard_map/broadcast_in_dim;reshape | solution.py:248
  771.2 57.9 %all-reduce.2.cloned.1.call-done = bf16[8,2,4,128,128]{3,4,1,2,0:T(8,128)(2,1)} async-done(((bf16[8,2,4,128,128]{3,4,1,2,0:T(8,128)(2,1)}), bf16[8,2,4,128,128]{3,4,1,2,0:T(8,128)(2,1)}) %all-reduce.2.cloned.1.call-update) | async-done | bytes 2097168 | tf_op jit(solution)/shard_map/psum | solution.py:243
  829.1 4.2 convert_multiply_fusion.2
  833.3 5.3 copy.55
  838.6 8.4 convert_multiply_fusion
  847.0 8.0 convert_multiply_fusion.1
  855.1 11.7 %pad_maximum_fusion = f32[2048,4096]{1,0:T(8,128)} fusion(f32[1024,4096]{1,0:T(8,128)S(1)} %convert_multiply_fusion, f32[1024,4096]{1,0:T(8,128)S(1)} %convert_multiply_fusion.1), kind=kLoop, calls=%fused_computation | loop fusion | flops 8388608 | bytes 67108864 | tf_op jit(solution)/shard_map/concatenate | solution.py:247
  (157 shorter events, 79.8 us)
Async XLA Ops:
  7.2 115.4 %all-gather.13.cloned.1.call-start = ((), (), s32[]{:S(2)}) async-start(), calls=%async_computation.1 | async-start | bytes 5242880 | tf_op jit(solution)/shard_map/all_gather | solution.py:165
  7.9 27.2 %collective-permute-start = (bf16[4,1024]{1,0:T(4,128)(2,1)S(1)}, bf16[4,1024]{1,0:T(4,128)(2,1)S(1)}, u32[]{:S(2)}, u32[]{:S(2)}) collective-permute-start(bf16[4,1024]{1,0:T(4,128)(2,1)S(1)} %slice_bitcast_fusion.4), channel_id=1, source_target_pairs={{2,0},{4,2},{6,4},{3,1},{5,3},{7,5},{10,8},{12,10},{14,12},{11,9},... | collective-permute-start | bytes 24584 | tf_op jit(solution)/shard_map/ppermute | solution.py:18
  12.5 20.0 %copy-start.15 = (bf16[4,4,128,2,128]{2,4,3,1,0:T(8,128)(2,1)}, bf16[4,4,128,2,128]{2,4,3,1,0:T(8,128)(2,1)S(1)}, u32[]{:S(2)}) copy-start(bf16[4,4,128,2,128]{2,4,3,1,0:T(8,128)(2,1)S(1)} %get-tuple-element.13) | copy-start | bytes 3145732
  12.5 25.4 %copy-start.13 = (bf16[4,4,128,2,128]{2,4,3,1,0:T(8,128)(2,1)}, bf16[4,4,128,2,128]{2,4,3,1,0:T(8,128)(2,1)S(1)}, u32[]{:S(2)}) copy-start(bf16[4,4,128,2,128]{2,4,3,1,0:T(8,128)(2,1)S(1)} %get-tuple-element.12) | copy-start | bytes 3145732
  37.8 165.6 %all-gather.11.cloned.1.call-start = ((), (), s32[]{:S(2)}) async-start(), calls=%async_computation | async-start | bytes 5242880 | tf_op jit(solution)/shard_map/all_gather | solution.py:165
  42.3 2.3 copy-start.22
  44.0 193.2 %all-gather.25.cloned.1.call-start = ((), (), s32[]{:S(2)}) async-start(), calls=%async_computation.8 | async-start | bytes 3145728 | tf_op jit(solution)/shard_map/all_gather | solution.py:167
  131.4 141.0 %all-gather.23.cloned.1.call-start = ((), (), s32[]{:S(2)}) async-start(), calls=%async_computation.7 | async-start | bytes 3145728 | tf_op jit(solution)/shard_map/all_gather | solution.py:167
  212.3 401.3 %all-gather.17.cloned.1.call-start = ((), (), s32[]{:S(2)}) async-start(), calls=%async_computation.3 | async-start | bytes 5242880 | tf_op jit(solution)/shard_map/all_gather | solution.py:203
  289.6 53.5 %copy-start.11 = (bf16[1024,1024]{1,0:T(8,128)(2,1)}, bf16[1024,1024]{1,0:T(8,128)(2,1)S(1)}, u32[]{:S(2)}) copy-start(bf16[1024,1024]{1,0:T(8,128)(2,1)S(1)} %get-tuple-element.10) | copy-start | bytes 6291460
  324.9 24.8 %collective-permute-start.12 = (bf16[512,4096]{1,0:T(8,128)(2,1)}, bf16[512,4096]{1,0:T(8,128)(2,1)}, u32[]{:S(2)}, u32[]{:S(2)}) collective-permute-start(bf16[512,4096]{1,0:T(8,128)(2,1)} %convolution_convert_fusion), channel_id=1, source_target_pairs={{0,8},{8,0},{16,24},{24,16},{1,9},{9,1},{17,25},{25,17},{2,10},{10... | collective-permute-start | bytes 12582920 | tf_op jit(solution)/shard_map/ppermute | solution.py:28
  324.9 12.3 %copy-start = (bf16[1024,4096]{1,0:T(8,128)(2,1)S(1)}, bf16[1024,4096]{1,0:T(8,128)(2,1)}, u32[]{:S(2)}) copy-start(bf16[1024,4096]{1,0:T(8,128)(2,1)} %fusion) | copy-start | bytes 25165828
  334.8 8.0 copy-start.9
  342.8 25.9 %collective-permute-start.3 = (bf16[512,1024]{1,0:T(8,128)(2,1)}, bf16[512,1024]{1,0:T(8,128)(2,1)}, u32[]{:S(2)}, u32[]{:S(2)}) collective-permute-start(bf16[512,1024]{1,0:T(8,128)(2,1)} %fusion.44), channel_id=1, source_target_pairs={{0,1},{1,0},{2,3},{3,2},{4,5},{5,4},{6,7},{7,6},{8,9},{9,8},{10,11... | collective-permute-start | bytes 3145736 | tf_op jit(solution)/shard_map/ppermute | solution.py:28
  343.1 6.6 copy-start.12
  349.5 62.0 %collective-permute-start.5 = (bf16[512,4096]{1,0:T(8,128)(2,1)}, bf16[512,4096]{1,0:T(8,128)(2,1)}, u32[]{:S(2)}, u32[]{:S(2)}) collective-permute-start(bf16[512,4096]{1,0:T(8,128)(2,1)} %convolution_convert_fusion.1), channel_id=1, source_target_pairs={{0,8},{8,0},{16,24},{24,16},{1,9},{9,1},{17,25},{25,17},{2,10},{10... | collective-permute-start | bytes 12582920 | tf_op jit(solution)/shard_map/ppermute | solution.py:28
  358.7 48.0 %collective-permute-start.13 = (bf16[256,4096]{1,0:T(8,128)(2,1)S(1)}, bf16[256,4096]{1,0:T(8,128)(2,1)}, u32[]{:S(2)}, u32[]{:S(2)}) collective-permute-start(bf16[256,4096]{1,0:T(8,128)(2,1)S(1)} %constant_dynamic-slice_fusion.1), channel_id=1, source_target_pairs={{0,16},{8,24},{16,0},{24,8},{1,17},{9,25},{17,1},{25,9},{2,18},{10... | collective-permute-start | bytes 6291464 | tf_op jit(solution)/shard_map/ppermute | solution.py:28
  379.1 244.8 %all-gather.21.cloned.1.call-start = ((), (), s32[]{:S(2)}) async-start(), calls=%async_computation.6 | async-start | bytes 2621440 | tf_op jit(solution)/shard_map/all_gather | solution.py:102
  409.7 27.4 %collective-permute-start.14 = (bf16[64,4096]{1,0:T(8,128)(2,1)S(1)}, bf16[64,4096]{1,0:T(8,128)(2,1)S(1)}, u32[]{:S(2)}, u32[]{:S(2)}) collective-permute-start(bf16[64,4096]{1,0:T(8,128)(2,1)S(1)} %constant_dynamic-slice_fusion), channel_id=1, source_target_pairs={{0,2},{2,4},{4,6},{6,0},{1,3},{3,5},{5,7},{7,1},{8,10},{10,12},{12... | collective-permute-start | bytes 1572872 | tf_op jit(solution)/shard_map/ppermute | solution.py:23
  424.6 55.1 %collective-permute-start.6 = (bf16[256,4096]{1,0:T(8,128)(2,1)}, bf16[256,4096]{1,0:T(8,128)(2,1)}, u32[]{:S(2)}, u32[]{:S(2)}) collective-permute-start(bf16[256,4096]{1,0:T(8,128)(2,1)} %constant_dynamic-slice_fusion.3), channel_id=1, source_target_pairs={{0,16},{8,24},{16,0},{24,8},{1,17},{9,25},{17,1},{25,9},{2,18},{10... | collective-permute-start | bytes 6291464 | tf_op jit(solution)/shard_map/ppermute | solution.py:28
  437.2 36.4 %collective-permute-start.15 = (bf16[64,4096]{1,0:T(8,128)(2,1)S(1)}, bf16[64,4096]{1,0:T(8,128)(2,1)S(1)}, u32[]{:S(2)}, u32[]{:S(2)}) collective-permute-start(bf16[64,4096]{1,0:T(8,128)(2,1)S(1)} %add_convert_fusion.8), channel_id=1, source_target_pairs={{0,2},{2,4},{4,6},{6,0},{1,3},{3,5},{5,7},{7,1},{8,10},{10,12},{12... | collective-permute-start | bytes 1572872 | tf_op jit(solution)/shard_map/ppermute | solution.py:23
  473.7 21.7 %collective-permute-start.16 = (bf16[64,4096]{1,0:T(8,128)(2,1)S(1)}, bf16[64,4096]{1,0:T(8,128)(2,1)S(1)}, u32[]{:S(2)}, u32[]{:S(2)}) collective-permute-start(bf16[64,4096]{1,0:T(8,128)(2,1)S(1)} %add_convert_fusion.7), channel_id=1, source_target_pairs={{0,2},{2,4},{4,6},{6,0},{1,3},{3,5},{5,7},{7,1},{8,10},{10,12},{12... | collective-permute-start | bytes 1572872 | tf_op jit(solution)/shard_map/ppermute | solution.py:23
  484.1 21.7 %collective-permute-start.7 = (bf16[64,4096]{1,0:T(8,128)(2,1)S(1)}, bf16[64,4096]{1,0:T(8,128)(2,1)S(1)}, u32[]{:S(2)}, u32[]{:S(2)}) collective-permute-start(bf16[64,4096]{1,0:T(8,128)(2,1)S(1)} %constant_dynamic-slice_fusion.2), channel_id=1, source_target_pairs={{0,2},{2,4},{4,6},{6,0},{1,3},{3,5},{5,7},{7,1},{8,10},{10,12},{12... | collective-permute-start | bytes 1572872 | tf_op jit(solution)/shard_map/ppermute | solution.py:23
  496.3 129.0 %all-gather.19.cloned.1.call-start = ((), (), s32[]{:S(2)}) async-start(), calls=%async_computation.5 | async-start | bytes 2621440 | tf_op jit(solution)/shard_map/all_gather | solution.py:102
  507.0 27.3 %collective-permute-start.8 = (bf16[64,4096]{1,0:T(8,128)(2,1)S(1)}, bf16[64,4096]{1,0:T(8,128)(2,1)S(1)}, u32[]{:S(2)}, u32[]{:S(2)}) collective-permute-start(bf16[64,4096]{1,0:T(8,128)(2,1)S(1)} %add_convert_fusion.11), channel_id=1, source_target_pairs={{0,2},{2,4},{4,6},{6,0},{1,3},{3,5},{5,7},{7,1},{8,10},{10,12},{12... | collective-permute-start | bytes 1572872 | tf_op jit(solution)/shard_map/ppermute | solution.py:23
  535.4 29.2 %collective-permute-start.9 = (bf16[64,4096]{1,0:T(8,128)(2,1)S(1)}, bf16[64,4096]{1,0:T(8,128)(2,1)S(1)}, u32[]{:S(2)}, u32[]{:S(2)}) collective-permute-start(bf16[64,4096]{1,0:T(8,128)(2,1)S(1)} %add_convert_fusion.10), channel_id=1, source_target_pairs={{0,2},{2,4},{4,6},{6,0},{1,3},{3,5},{5,7},{7,1},{8,10},{10,12},{12... | collective-permute-start | bytes 1572872 | tf_op jit(solution)/shard_map/ppermute | solution.py:23
  566.6 125.3 %all-gather.15.cloned.1.call-start = ((), (), s32[]{:S(2)}) async-start(), calls=%async_computation.2 | async-start | bytes 5242880 | tf_op jit(solution)/shard_map/all_gather | solution.py:203
  576.1 34.6 %copy-start.23 = (s32[1,4096]{1,0:T(1,128)S(1)}, s32[1,4096]{1,0:T(1,128)}, u32[]{:S(2)}) copy-start(s32[1,4096]{1,0:T(1,128)} %param.11) | copy-start | bytes 49156
  576.1 34.7 %copy-start.6 = (bf16[1024,4,128]{0,2,1:T(8,128)(2,1)S(1)}, bf16[1024,4,128]{0,2,1:T(8,128)(2,1)}, u32[]{:S(2)}) copy-start(bf16[1024,4,128]{0,2,1:T(8,128)(2,1)} %fusion.32) | copy-start | bytes 3145732
  576.1 35.2 %copy-start.7 = (bf16[1024,4,128]{0,2,1:T(8,128)(2,1)S(1)}, bf16[1024,4,128]{0,2,1:T(8,128)(2,1)}, u32[]{:S(2)}) copy-start(bf16[1024,4,128]{0,2,1:T(8,128)(2,1)} %fusion.34) | copy-start | bytes 3145732
  576.1 24.0 %collective-permute-start.1 = (bf16[512,1024]{1,0:T(8,128)(2,1)S(1)}, bf16[512,1024]{1,0:T(8,128)(2,1)S(1)}, u32[]{:S(2)}, u32[]{:S(2)}) collective-permute-start(bf16[512,1024]{1,0:T(8,128)(2,1)S(1)} %fusion.38), channel_id=1, source_target_pairs={{0,1},{1,0},{2,3},{3,2},{4,5},{5,4},{6,7},{7,6},{8,9},{9,8},{10,11... | collective-permute-start | bytes 3145736 | tf_op jit(solution)/shard_map/ppermute | solution.py:28
  610.4 218.7 %all-reduce.2.cloned.1.call-start = ((), (), s32[]{:S(2)}) async-start(), calls=%async_computation.4 | async-start | bytes 4194304 | tf_op jit(solution)/shard_map/psum | solution.py:243
  610.8 2.8 copy-start.25
  610.8 2.8 copy-start.27
  622.1 101.1 %collective-permute-start.4 = (bf16[1,512]{1,0:T(2,128)(2,1)S(1)}, bf16[1,512]{1,0:T(2,128)(2,1)S(1)}, u32[]{:S(2)}, u32[]{:S(2)}) collective-permute-start(bf16[1,512]{1,0:T(2,128)(2,1)S(1)} %slice.148), channel_id=1, source_target_pairs={{0,2},{2,4},{4,6},{1,3},{3,5},{5,7},{8,10},{10,12},{12,14},{9,11},... | collective-permute-start | bytes 3080 | tf_op jit(solution)/shard_map/ppermute | solution.py:18
  623.9 76.6 %copy-start.17 = (bf16[256,4096]{1,0:T(8,128)(2,1)S(1)}, bf16[256,4096]{1,0:T(8,128)(2,1)}, u32[]{:S(2)}) copy-start(bf16[256,4096]{1,0:T(8,128)(2,1)} %all-gather.21.cloned.1.call-done) | copy-start | bytes 6291460
  623.9 76.6 %collective-permute-start.17 = (bf16[256,4096]{1,0:T(8,128)(2,1)}, bf16[256,4096]{1,0:T(8,128)(2,1)}, u32[]{:S(2)}, u32[]{:S(2)}) collective-permute-start(bf16[256,4096]{1,0:T(8,128)(2,1)} %all-gather.21.cloned.1.call-done), channel_id=1, source_target_pairs={{0,16},{8,24},{16,0},{24,8},{1,17},{9,25},{17,1},{25,9},{2,18},{10... | collective-permute-start | bytes 6291464 | tf_op jit(solution)/shard_map/ppermute | solution.py:28
  625.4 89.5 %collective-permute-start.10 = (bf16[256,4096]{1,0:T(8,128)(2,1)}, bf16[256,4096]{1,0:T(8,128)(2,1)}, u32[]{:S(2)}, u32[]{:S(2)}) collective-permute-start(bf16[256,4096]{1,0:T(8,128)(2,1)} %all-gather.19.cloned.1.call-done), channel_id=1, source_target_pairs={{0,16},{8,24},{16,0},{24,8},{1,17},{9,25},{17,1},{25,9},{2,18},{10... | collective-permute-start | bytes 6291464 | tf_op jit(solution)/shard_map/ppermute | solution.py:28
  700.4 14.4 %copy-start.18 = (bf16[256,4096]{1,0:T(8,128)(2,1)S(1)}, bf16[256,4096]{1,0:T(8,128)(2,1)}, u32[]{:S(2)}) copy-start(bf16[256,4096]{1,0:T(8,128)(2,1)} %all-gather.19.cloned.1.call-done) | copy-start | bytes 6291460
  705.3 133.3 %collective-permute-start.18 = (bf16[512,4096]{1,0:T(8,128)(2,1)}, bf16[512,4096]{1,0:T(8,128)(2,1)}, u32[]{:S(2)}, u32[]{:S(2)}) collective-permute-start(bf16[512,4096]{1,0:T(8,128)(2,1)} %maximum_select_fusion.3), channel_id=1, source_target_pairs={{0,8},{8,0},{16,24},{24,16},{1,9},{9,1},{17,25},{25,17},{2,10},{10... | collective-permute-start | bytes 12582920 | tf_op jit(solution)/shard_map/ppermute | solution.py:28
  705.5 19.0 %copy-start.19 = (bf16[1024,4,128]{2,0,1:T(8,128)(2,1)}, bf16[1024,4,128]{2,0,1:T(8,128)(2,1)S(1)}, u32[]{:S(2)}) copy-start(bf16[1024,4,128]{2,0,1:T(8,128)(2,1)S(1)} %copy_bitcast_fusion.1) | copy-start | bytes 3145732
  719.6 4.9 copy-start.5
  719.7 127.4 %collective-permute-start.11 = (bf16[512,4096]{1,0:T(8,128)(2,1)}, bf16[512,4096]{1,0:T(8,128)(2,1)}, u32[]{:S(2)}, u32[]{:S(2)}) collective-permute-start(bf16[512,4096]{1,0:T(8,128)(2,1)} %maximum_select_fusion.2), channel_id=1, source_target_pairs={{0,8},{8,0},{16,24},{24,16},{1,9},{9,1},{17,25},{25,17},{2,10},{10... | collective-permute-start | bytes 12582920 | tf_op jit(solution)/shard_map/ppermute | solution.py:28
  719.8 6.2 copy-start.20
  719.9 4.4 collective-permute-start.2
  724.5 2.2 copy-start.3
  729.9 4.7 copy-start.14
  729.9 4.7 copy-start.21
  (9 other events, 13.9 us)
Sparse Core Ops, SparseCore 0:
  38.0 84.5 all-gather.12
  124.1 79.2 all-gather.10
  205.6 31.6 all-gather.24
  239.2 33.1 all-gather.22
  379.2 103.0 all-gather.16
  496.5 62.3 all-gather.20
  566.7 44.0 all-gather.18
  612.4 79.4 all-gather.14
  730.0 99.0 all-reduce.1

commit v2 on v1

--- a/solution.py
+++ b/solution.py
@@ -16,11 +16,6 @@
     devices = range(lax.axis_size(axis))
     route = [(i - distance, i) for i in devices if i - distance in devices]
     return lax.ppermute(block, axis, route)
-
-
-def ring(block, axis):
-    count = lax.axis_size(axis)
-    return lax.ppermute(block, axis, [(i, (i + 1) % count) for i in range(count)])
 
 
 def swapped(block, axis, bit):
@@ -70,36 +65,28 @@
     return (a.astype(F32) + b.astype(F32)).astype(BF16)
 
 
-def summed_product(rows_t, right):
-    dp_count = lax.axis_size("dp")
+def bit_list(axis):
+    return [1 << i for i in range(lax.axis_size(axis).bit_length() - 1)]
+
+
+def product(columns, right):
+    return lax.dot_general(
+        columns, right, (((0,), (0,)), ((), ())), preferred_element_type=F32
+    )
+
+
+def column_half(rows_t, which):
+    half = rows_t.shape[1] // 2
+    return lax.dynamic_slice_in_dim(rows_t, which * half, half, 1)
+
+
+def summed_rest(held):
     dp_rank = lax.axis_index("dp")
-    seq_count = lax.axis_size("seq")
-    seq_rank = lax.axis_index("seq")
-    bits = [1 << i for i in range(dp_count.bit_length() - 1)]
-
-    def product(columns):
-        return lax.dot_general(
-            columns, right, (((0,), (0,)), ((), ())), preferred_element_type=F32
-        )
-
-    half = rows_t.shape[1] // 2
-    own = dp_rank % 2
-    send = product(lax.dynamic_slice_in_dim(rows_t, (1 - own) * half, half, 1)).astype(BF16)
-    got = swapped(send, "dp", 1)
-    mine = product(lax.dynamic_slice_in_dim(rows_t, own * half, half, 1))
-    held = (mine + got.astype(F32)).astype(BF16)
-    for bit in bits[1:]:
+    bits = bit_list("dp")[1:]
+    for bit in bits:
         keep, give = halves(held, dp_rank // bit % 2)
         held = added(keep, swapped(give, "dp", bit))
-    depth = held.shape[0] // seq_count
-
-    def part(index):
-        return lax.dynamic_slice_in_dim(held, (index + seq_count) % seq_count * depth, depth, 0)
-
-    moving = part(seq_rank - 1)
-    for step in range(seq_count - 1):
-        moving = added(ring(moving, "seq"), part(seq_rank - 2 - step))
-    held = lax.all_gather(moving, "seq", axis=0, tiled=True)
+    held = lax.psum(held, "seq")
     for bit in bits[::-1]:
         held = rejoined(held, swapped(held, "dp", bit), dp_rank // bit % 2)
     return held
@@ -149,6 +136,8 @@
     per = groups_here // forward_chunks
     down_parts = []
     gathered_parts = []
+    pooled_parts = []
+    got_parts = []
     for chunk in range(forward_chunks):
         sel = slice(chunk * per, (chunk + 1) * per)
         both = jnp.einsum(
@@ -164,9 +153,22 @@
         down_parts.append(part)
         whole = lax.all_gather(part, "seq", axis=0, tiled=True)
         pooled = jnp.dot(token_weight, whole, preferred_element_type=F32).astype(BF16)
-        gathered_parts.append(lax.all_gather(pooled, "tensor", axis=1, tiled=False))
+        if tensor_count == 2:
+            got = swapped(pooled, "tensor", 1)
+            pooled_parts.append(pooled)
+            got_parts.append(got)
+        else:
+            gathered_parts.append(lax.all_gather(pooled, "tensor", axis=1, tiled=False))
     downsampled = jnp.concatenate(down_parts, axis=1)
-    gathered = jnp.concatenate(gathered_parts, axis=2).reshape(tokens, tensor_count * width)
+    if tensor_count == 2:
+        gathered = jnp.where(
+            tensor_rank == 0,
+            jnp.concatenate(pooled_parts + got_parts, axis=1),
+            jnp.concatenate(got_parts + pooled_parts, axis=1),
+        )
+    else:
+        gathered = jnp.concatenate(gathered_parts, axis=2)
+        gathered = gathered.reshape(tokens, tensor_count * width)
 
     predicted = jnp.dot(gathered, proj_weight, preferred_element_type=F32)
     err_grad = (predicted - teacher[0].astype(F32)).astype(BF16)
@@ -200,51 +202,59 @@
                 scatter_dimension=0,
                 tiled=True,
             )
-        token_grads.append(lax.all_gather(pooled_grad_t, "seq", axis=1, tiled=True))
-
+        token_grads.append(pooled_grad_t)
+
+    dp_rank = lax.axis_index("dp")
+    own = dp_rank % 2
     chunk_rows = gathered.shape[1] // PROJ_CHUNKS
     token_scale = 1.0 / jnp.sqrt(F32(dp_count * tokens_all))
-    proj_parts = [
-        summed_product(gathered[:, i * chunk_rows : (i + 1) * chunk_rows], err_grad)
-        for i in range(PROJ_CHUNKS)
+    chunks = [gathered[:, i * chunk_rows : (i + 1) * chunk_rows] for i in range(PROJ_CHUNKS)]
+    sends = [product(column_half(c, 1 - own), err_grad).astype(BF16) for c in chunks]
+    sends, token_grads = lax.optimization_barrier((sends, token_grads))
+    token_grads = [lax.all_gather(t, "seq", axis=1, tiled=True) for t in token_grads]
+    proj_grad = jnp.zeros((gathered.shape[1], err_grad.shape[1]), F32)
+    for i in range(PROJ_CHUNKS):
+        mine = product(column_half(chunks[i], own), err_grad)
+        held = (mine + swapped(sends[i], "dp", 1).astype(F32)).astype(BF16)
+        held = summed_rest(held)
+        other = swapped(held, "dp", 1)
+        for block, which in ((held, own), (other, 1 - own)):
+            proj_grad = lax.dynamic_update_slice_in_dim(
+                proj_grad,
+                block.astype(F32) * token_scale,
+                i * chunk_rows + which * (chunk_rows // 2),
+                0,
+            )
+
+    position_scale = 1.0 / jnp.sqrt(F32(dp_count * positions * seq_count))
+    down_parts = [
+        lax.dot_general(
+            local_weight, whole, (((0,), (1,)), ((), ())), preferred_element_type=F32
+        ).astype(BF16)
+        for whole in token_grads
     ]
-
-    position_scale = 1.0 / jnp.sqrt(F32(dp_count * positions * seq_count))
-    byte_parts = []
-    conv_parts = []
-    for chunk in range(backward_chunks):
-        sel = slice(chunk * per, (chunk + 1) * per)
-        down = lax.dot_general(
-            local_weight,
-            token_grads[chunk],
-            (((0,), (1,)), ((), ())),
-            preferred_element_type=F32,
-        ).astype(BF16)
-        before = shifted(down[-1:], "seq", 1)
-        earlier = jnp.concatenate([before, down[:-1]], axis=0)
-        pair = jnp.concatenate(
-            [
-                down.reshape(positions, per, group_width),
-                earlier.reshape(positions, per, group_width),
-            ],
-            axis=2,
-        )
-        grads = jnp.einsum(
-            "pkgc,pgn->gkcn", blocks[:, :, sel], pair, preferred_element_type=F32
-        )
-        grads = grads.reshape(per, STRIDE, group_width, 2, group_width)
-        conv_parts.append(jnp.transpose(grads, (0, 3, 1, 2, 4)))
-        part = jnp.einsum(
-            "pgn,gkcn->pkgc", pair, taps_pair[sel], preferred_element_type=F32
-        )
-        byte_parts.append(part.astype(BF16))
-    byte_grad = jnp.concatenate(byte_parts, axis=2).reshape(row_total, width)
-    conv_local = jnp.concatenate(conv_parts, axis=0)
-    conv_summed = lax.psum(conv_local.astype(BF16), ("dp", "seq")).astype(F32)
-    conv_grad = (conv_summed * position_scale).reshape(
+    down = jnp.concatenate(down_parts, axis=1)
+    before = shifted(down[-1:], "seq", 1)
+    earlier = jnp.concatenate([before, down[:-1]], axis=0)
+    pair = jnp.concatenate(
+        [
+            down.reshape(positions, groups_here, group_width),
+            earlier.reshape(positions, groups_here, group_width),
+        ],
+        axis=2,
+    )
+    grads = jnp.einsum("pkgc,pgn->gkcn", blocks, pair, preferred_element_type=F32)
+    grads = grads.astype(BF16).reshape(-1, 2 * group_width)
+    keep, give = halves(grads, own)
+    held = summed_rest(added(keep, swapped(give, "dp", 1)))
+    grads = rejoined(held, swapped(held, "dp", 1), own).astype(F32) * position_scale
+    grads = grads.reshape(groups_here, STRIDE, group_width, 2, group_width)
+    conv_grad = jnp.transpose(grads, (0, 3, 1, 2, 4)).reshape(
         groups_here, KERNEL * group_width, group_width
     )
-    proj_grad = jnp.concatenate([p.astype(F32) * token_scale for p in proj_parts], axis=0)
+    byte_grad = jnp.einsum(
+        "pgn,gkcn->pkgc", pair, taps_pair, preferred_element_type=F32
+    ).astype(BF16).reshape(row_total, width)
     return (downsampled[None], byte_grad[None], conv_grad, proj_grad)
 
 

time: 882 us -> 933 us (1.058)
  waiting for transfers between devices: 503 us -> 576 us
  starting transfers between devices: 42.3 us -> 17.9 us
  other arithmetic: 76 us -> 57.7 us
  matrix products: 145 us -> 155 us
  local copies, waits for them, and re-layouts: 93 us -> 103 us
    psum x1, waiting for transfers between devices: 57.9 us -> 174 us  [summed_rest(): held = lax.psum(held, 'seq')]
    ppermute x6 -> x0, waiting for transfers between devices: 106 us -> none  [ring(): lax.ppermute(block, axis, [(i, (i + 1) % count) for i in range(count)])]
    ppermute x10 -> x16, waiting for transfers between devices: 67.7 us -> 136 us  [swapped(): return lax.ppermute(block, axis, [(i, i ^ bit) for i in range(count)])]
    dynamic_update_slice x0 -> x4, other arithmetic: none -> 28.5 us  [local(): lax.dynamic_update_slice_in_dim(proj_grad, block.astype(F32) * token_scal...]
    ppermute x6 -> x0, starting transfers between devices: 26.9 us -> none  [ring(): lax.ppermute(block, axis, [(i, (i + 1) % count) for i in range(count)])]
    concatenate x4, other arithmetic: 28.3 us -> 5.15 us  [the longest x1 2.64 us: local(): earlier = jnp.concatenate([before, down[:-1]], axis=0)]
    mul x3 -> x1, other arithmetic: 20.6 us -> 4.13 us  [local(): rejoined(held, swapped(held, 'dp', 1), own).astype(F32) * position_scale]
    concatenate x1 -> x0, local copies, waits for them, and re-layouts: 12.4 us -> none  [local(): byte_grad = jnp.concatenate(byte_parts, axis=2).reshape(row_total, width)]
  transfers between devices with their start and end apart: 28 -> 23, of which waited for: 17 -> 14; matrix products, arithmetic and copies ran while one was open for 26% -> 24% of each run, Pallas kernels for 0% -> 0%
where the time goes in v2:
time: 933 us; the launch traced here: 925 us
  waiting for transfers between devices  576 us (62%)
  matrix products  155 us (17%)
  local copies, waits for them, and re-layouts  103 us (11%)
  other arithmetic  57.7 us (6%)
  starting transfers between devices  17.9 us (2%)
  between operations  14.4 us (2%)
    psum x1, waiting for transfers between devices, summed_rest(): held = lax.psum(held, 'seq')  174 us
    all_gather x2, waiting for transfers between devices, local(): whole = lax.all_gather(part, 'seq', axis=0, tiled=True)  147 us
    ppermute x16, waiting for transfers between devices, swapped(): return lax.ppermute(block, axis, [(i, i ^ bit) for i in range(count)])  136 us
    all_gather x2, waiting for transfers between devices, local(): lax.all_gather(t, 'seq', axis=1, tiled=True)  118 us
    dot_general x4, matrix products, back(): lax.dot_general(lax.dynamic_index_in_dim(weight_part, block, 0, keepdims=...  38.5 us
    dot_general x4, matrix products, product(): lax.dot_general(columns, right, (((0,), (0,)), ((), ())), preferred_eleme...  34.3 us
    dynamic_update_slice x4, other arithmetic, local(): lax.dynamic_update_slice_in_dim(proj_grad, block.astype(F32) * token_scal...  28.5 us
    dot_general x1, matrix products, local(): predicted = jnp.dot(gathered, proj_weight, preferred_element_type=F32)  25.2 us
  transfers between devices with their start and end apart: 23, of which 14 were waited for; matrix products, arithmetic and copies ran while one was open for 24% of the time, Pallas kernels for 0%

profile of v2, /device:TPU:0, one launch (start us, length us, event | category | flops | bytes accessed | tf_op | source)
XLA Modules:
  0.0 924.5 jit_solution(12934587252552101641)
XLA Ops:
  9.2 3.0 copy.31
  12.5 8.9 copy.55
  21.4 10.2 %fusion.89 = (bf16[1024,4,4,128]{3,2,1,0:T(4,128)(2,1)S(1)}, bf16[1024,4,4,128]{3,2,1,0:T(4,128)(2,1)}) fusion(bf16[1024,4,8,128]{3,2,1,0:T(8,128)(2,1)} %bitcast.132), kind=kLoop, calls=%fused_computation.125 | loop fusion | bytes 16777216 | tf_op jit(solution)/shard_map/slice | solution.py:144
  36.7 3.8 fusion.26
  45.0 76.3 %all-gather.5.cloned.1.call-done = bf16[4096,512]{0,1:T(8,128)(2,1)} async-done(((bf16[1024,512]{0,1:T(8,128)(2,1)}), bf16[4096,512]{0,1:T(8,128)(2,1)}) %all-gather.5.cloned.1.call-update) | async-done | bytes 4194320 | tf_op jit(solution)/shard_map/all_gather | solution.py:154
  121.3 8.5 fusion.53
  131.3 70.9 %all-gather.7.cloned.1.call-done = bf16[4096,512]{0,1:T(8,128)(2,1)} async-done(((bf16[1024,512]{0,1:T(8,128)(2,1)}), bf16[4096,512]{0,1:T(8,128)(2,1)}) %all-gather.7.cloned.1.call-update) | async-done | bytes 4194320 | tf_op jit(solution)/shard_map/all_gather | solution.py:154
  202.2 8.6 fusion.54
  212.4 11.7 %fusion.88 = (bf16[2,512,4096]{2,1,0:T(8,128)(2,1)}, bf16[2,512,4096]{2,1,0:T(8,128)(2,1)}) fusion(bf16[2,1024,4096]{2,1,0:T(8,128)(2,1)} %bitcast.134), kind=kLoop, calls=%fused_computation.124 | loop fusion | bytes 33554432 | tf_op jit(solution)/shard_map/slice | solution.py:181
  224.1 11.7 %collective-permute-done.2 = bf16[1024,512]{0,1:T(8,128)(2,1)S(1)} collective-permute-done((bf16[1024,512]{0,1:T(8,128)(2,1)S(1)}, bf16[1024,512]{0,1:T(8,128)(2,1)S(1)}, u32[]{:S(2)}, u32[]{:S(2)}) %collective-permute-start.2) | collective-permute-done | bytes 1048608 | tf_op jit(solution)/shard_map/ppermute | solution.py:23
  239.9 25.2 %fusion = bf16[1024,4096]{1,0:T(8,128)(2,1)} fusion(bf16[1024,2048]{0,1:T(8,128)(2,1)S(1)} %maximum_select_fusion, bf16[2048,4096]{1,0:T(8,128)(2,1)} %param.9, bf16[1,1024,4096]{2,1,0:T(8,128)(2,1)} %param.10), kind=kOutput, calls=%fused_computation.1 | convolution fusion | flops 17192452096 | bytes 37748736 | tf_op jit(solution)/shard_map/dot_general | solution.py:173
  265.1 9.2 fusion.48
  275.9 10.3 %fusion.42 = bf16[512,1024]{1,0:T(8,128)(2,1)} fusion(bf16[1024,4096]{1,0:T(8,128)(2,1)} %fusion, bf16[2,512,4096]{2,1,0:T(8,128)(2,1)} %get-tuple-element.22, s32[]{:T(128)S(6)} %select_n.138), kind=kOutput, calls=%fused_computation.67 | convolution fusion | flops 4295491584 | bytes 13631492 | tf_op jit(solution)/shard_map/dot_general | solution.py:184
  286.7 9.6 %convolution_convert_fusion = bf16[512,4096]{1,0:T(8,128)(2,1)} fusion(bf16[1024,4096]{1,0:T(8,128)(2,1)} %fusion, bf16[1024,1024]{0,1:T(8,128)(2,1)S(1)} %copy-done.11, s32[]{:T(128)S(6)} %select_n.136), kind=kOutput, calls=%fused_computation.17 | convolution fusion | flops 4297064448 | bytes 13631492 | tf_op jit(solution)/shard_map/dot_general | solution.py:73
  296.4 6.1 convolution_convert_fusion.1
  302.4 8.7 add_convert_fusion.5
  311.1 9.9 %collective-permute-done.3 = bf16[512,1024]{1,0:T(8,128)(2,1)} collective-permute-done((bf16[512,1024]{1,0:T(8,128)(2,1)}, bf16[512,1024]{1,0:T(8,128)(2,1)}, u32[]{:S(2)}, u32[]{:S(2)}) %collective-permute-start.3) | collective-permute-done | bytes 1048608 | tf_op jit(solution)/shard_map/ppermute | solution.py:23
  321.0 10.3 %add_convert_fusion.6 = bf16[512,1024]{1,0:T(8,128)(2,1)} fusion(bf16[512,1024]{1,0:T(8,128)(2,1)} %collective-permute-done.3, bf16[1024,4096]{1,0:T(8,128)(2,1)} %fusion, bf16[2,512,4096]{2,1,0:T(8,128)(2,1)} %get-tuple-element.22, s32[]{:T(128)S(6)} %select_n.137), kind=kOutput, calls=%fused_computation.63 | convolution fusion | flops 4297588736 | bytes 14680068 | tf_op jit(solution)/shard_map/dot_general | solution.py:184
  332.1 6.9 collective-permute-done.14
  339.0 9.7 %add_convert_fusion = bf16[512,4096]{1,0:T(8,128)(2,1)S(1)} fusion(bf16[512,4096]{1,0:T(8,128)(2,1)} %collective-permute-done.14, bf16[1024,4096]{1,0:T(8,128)(2,1)} %fusion, bf16[1024,1024]{0,1:T(8,128)(2,1)} %get-tuple-element.25, s32[]{:T(128)S(6)} %select_n.150), kind=kOutput, calls=%fused_computation.8 | convolution fusion | flops 4301258752 | bytes 17825796 | tf_op jit(solution)/shard_map/dot_general | solution.py:73
  352.0 8.9 add_convert_fusion.1
  365.5 45.7 %all-gather.11.cloned.1.call-done = bf16[512,4096]{1,0:T(8,128)(2,1)} async-done(((bf16[512,1024]{1,0:T(8,128)(2,1)}), bf16[512,4096]{1,0:T(8,128)(2,1)}) %all-gather.11.cloned.1.call-update) | async-done | bytes 4194320 | tf_op jit(solution)/shard_map/all_gather | solution.py:214
  411.2 8.4 fusion.51
  419.5 72.4 %all-gather.9.cloned.1.call-done = bf16[512,4096]{1,0:T(8,128)(2,1)} async-done(((bf16[512,1024]{1,0:T(8,128)(2,1)}), bf16[512,4096]{1,0:T(8,128)(2,1)}) %all-gather.9.cloned.1.call-update) | async-done | bytes 4194320 | tf_op jit(solution)/shard_map/all_gather | solution.py:214
  491.9 8.8 fusion.52
  504.5 3.9 copy.38
  511.6 4.0 copy.39
  515.6 10.2 %fusion.36 = bf16[8,256,4,128]{1,3,2,0:T(8,128)(2,1)S(1)} fusion(bf16[1024,4,8,128]{3,2,1,0:T(8,128)(2,1)} %bitcast.133, bf16[1024,8,128]{2,0,1:T(8,128)(2,1)} %copy.39, bf16[1024,8,128]{2,0,1:T(8,128)(2,1)} %copy.38), kind=kOutput, calls=%fused_computation.65 | convolution fusion | flops 2156920832 | bytes 14680064 | tf_op jit(solution)/shard_map/pkgc,pgn->gkcn/dot_general | solution.py:246
  526.1 4.5 add_convert_fusion.2
  533.6 3.7 add_convert_fusion.3
  537.3 9.1 collective-permute-done.7
  547.4 174.1 %all-reduce.3.cloned.1.call-done = (bf16[1024,256]{1,0:T(8,128)(2,1)}, bf16[256,4096]{1,0:T(8,128)(2,1)}, bf16[256,4096]{1,0:T(8,128)(2,1)}) async-done(((bf16[1024,256]{1,0:T(8,128)(2,1)}, bf16[256,4096]{1,0:T(8,128)(2,1)}, bf16[256,4096]{1,0:T(8,128)(2,1)}), (bf16[1024,256]{1,0:T(8,128)(2,1)}, bf16[256,4096]{1,0:T(8,128)(2,1)}, bf16[256,4096]{1,0:T(8,128)(2,1)})) %all-reduce.3.cloned.1.call-update) | async-done | bytes 4718608 | tf_op jit(solution)/shard_map/psum | solution.py:89
  723.0 46.1 %collective-permute-done.12 = bf16[256,4096]{1,0:T(8,128)(2,1)S(1)} collective-permute-done((bf16[256,4096]{1,0:T(8,128)(2,1)}, bf16[256,4096]{1,0:T(8,128)(2,1)S(1)}, u32[]{:S(2)}, u32[]{:S(2)}) %collective-permute-start.12) | collective-permute-done | bytes 2097184 | tf_op jit(solution)/shard_map/ppermute | solution.py:23
  770.4 11.4 %broadcast_in_dim.71 = f32[2048,4096]{1,0:T(8,128)} broadcast(f32[]{:T(128)} %constant.96.clone.1), dimensions={} | broadcast | bytes 33554436 | tf_op jit(solution)/shard_map/broadcast_in_dim | solution.py:215
  781.9 7.6 multiply_dynamic-update-slice_fusion.3
  791.1 5.9 collective-permute-done.13
  797.1 6.7 multiply_dynamic-update-slice_fusion.2
  803.8 34.0 %collective-permute-done.16 = bf16[256,4096]{1,0:T(8,128)(2,1)} collective-permute-done((bf16[256,4096]{1,0:T(8,128)(2,1)S(1)}, bf16[256,4096]{1,0:T(8,128)(2,1)}, u32[]{:S(2)}, u32[]{:S(2)}) %collective-permute-start.16) | collective-permute-done | bytes 2097184 | tf_op jit(solution)/shard_map/ppermute | solution.py:23
  837.8 7.5 multiply_dynamic-update-slice_fusion.1
  846.8 12.8 %collective-permute-done.8 = bf16[1024,256]{1,0:T(8,128)(2,1)S(1)} collective-permute-done((bf16[1024,256]{1,0:T(8,128)(2,1)S(1)}, bf16[1024,256]{1,0:T(8,128)(2,1)S(1)}, u32[]{:S(2)}, u32[]{:S(2)}) %collective-permute-start.8) | collective-permute-done | bytes 524320 | tf_op jit(solution)/shard_map/ppermute | solution.py:23
  861.8 3.0 maximum_bitcast_fusion.3
  864.9 6.3 convert_bitcast_fusion
  871.1 12.1 %copy.41 = bf16[1024,4,8,128]{3,2,1,0:T(8,128)(2,1)} copy(bf16[1024,4,8,128]{3,0,1,2:T(8,128)(2,1)} %convert_bitcast_fusion) | data formatting | bytes 16777216 | tf_op jit(solution)/shard_map/convert_element_type | solution.py:257
  883.2 13.3 %broadcast_in_dim_reshape.4 = bf16[1,4096,1024]{2,1,0:T(8,128)(2,1)} reshape(bf16[1024,4,8,128]{3,2,1,0:T(8,128)(2,1)} %copy.41) | data formatting | bytes 16777216 | tf_op jit(solution)/shard_map/broadcast_in_dim;reshape | solution.py:258
  896.5 4.1 convert_multiply_fusion
  900.6 5.7 mul.100
  906.4 4.8 copy.43
  911.1 6.7 multiply_dynamic-update-slice_fusion
  (121 shorter events, 48.8 us)
Async XLA Ops:
  7.2 114.1 %all-gather.5.cloned.1.call-start = ((), (), s32[]{:S(2)}) async-start(), calls=%async_computation | async-start | bytes 5242880 | tf_op jit(solution)/shard_map/all_gather | solution.py:154
  7.9 26.0 %collective-permute-start = (bf16[4,1024]{1,0:T(4,128)(2,1)S(1)}, bf16[4,1024]{1,0:T(4,128)(2,1)S(1)}, u32[]{:S(2)}, u32[]{:S(2)}) collective-permute-start(bf16[4,1024]{1,0:T(4,128)(2,1)S(1)} %slice_bitcast_fusion.4), channel_id=1, source_target_pairs={{2,0},{4,2},{6,4},{3,1},{5,3},{7,5},{10,8},{12,10},{14,12},{11,9},... | collective-permute-start | bytes 24584 | tf_op jit(solution)/shard_map/ppermute | solution.py:18
  31.6 1.6 copy-start.18
  33.3 1.6 copy-start.2
  36.6 165.6 %all-gather.7.cloned.1.call-start = ((), (), s32[]{:S(2)}) async-start(), calls=%async_computation.1 | async-start | bytes 5242880 | tf_op jit(solution)/shard_map/all_gather | solution.py:154
  41.1 2.3 copy-start.13
  42.8 368.3 %all-gather.11.cloned.1.call-start = ((), (), s32[]{:S(2)}) async-start(), calls=%async_computation.3 | async-start | bytes 5242880 | tf_op jit(solution)/shard_map/all_gather | solution.py:214
  44.3 0.6 copy-start.16
  44.3 0.6 copy-start.14
  129.8 94.3 %collective-permute-start.1 = (bf16[1024,512]{0,1:T(8,128)(2,1)S(1)}, bf16[1024,512]{0,1:T(8,128)(2,1)S(1)}, u32[]{:S(2)}, u32[]{:S(2)}) collective-permute-start(bf16[1024,512]{0,1:T(8,128)(2,1)S(1)} %fusion.53), channel_id=1, source_target_pairs={{0,1},{1,0},{2,3},{3,2},{4,5},{5,4},{6,7},{7,6},{8,9},{9,8},{10,11... | collective-permute-start | bytes 3145736 | tf_op jit(solution)/shard_map/ppermute | solution.py:23
  210.8 25.0 %collective-permute-start.2 = (bf16[1024,512]{0,1:T(8,128)(2,1)S(1)}, bf16[1024,512]{0,1:T(8,128)(2,1)S(1)}, u32[]{:S(2)}, u32[]{:S(2)}) collective-permute-start(bf16[1024,512]{0,1:T(8,128)(2,1)S(1)} %fusion.54), channel_id=1, source_target_pairs={{0,1},{1,0},{2,3},{3,2},{4,5},{5,4},{6,7},{7,6},{8,9},{9,8},{10,11... | collective-permute-start | bytes 3145736 | tf_op jit(solution)/shard_map/ppermute | solution.py:23
  274.3 28.1 %collective-permute-start.4 = (bf16[512,1024]{1,0:T(8,128)(2,1)S(1)}, bf16[512,1024]{1,0:T(8,128)(2,1)S(1)}, u32[]{:S(2)}, u32[]{:S(2)}) collective-permute-start(bf16[512,1024]{1,0:T(8,128)(2,1)S(1)} %fusion.48), channel_id=1, source_target_pairs={{0,1},{1,0},{2,3},{3,2},{4,5},{5,4},{6,7},{7,6},{8,9},{9,8},{10,11... | collective-permute-start | bytes 3145736 | tf_op jit(solution)/shard_map/ppermute | solution.py:23
  275.9 10.9 %copy-start.11 = (bf16[1024,1024]{0,1:T(8,128)(2,1)S(1)}, bf16[1024,1024]{0,1:T(8,128)(2,1)}, u32[]{:S(2)}) copy-start(bf16[1024,1024]{0,1:T(8,128)(2,1)} %get-tuple-element.25) | copy-start | bytes 6291460
  286.2 34.8 %collective-permute-start.3 = (bf16[512,1024]{1,0:T(8,128)(2,1)}, bf16[512,1024]{1,0:T(8,128)(2,1)}, u32[]{:S(2)}, u32[]{:S(2)}) collective-permute-start(bf16[512,1024]{1,0:T(8,128)(2,1)} %fusion.42), channel_id=1, source_target_pairs={{0,1},{1,0},{2,3},{3,2},{4,5},{5,4},{6,7},{7,6},{8,9},{9,8},{10,11... | collective-permute-start | bytes 3145736 | tf_op jit(solution)/shard_map/ppermute | solution.py:23
  286.7 9.6 %copy-start.19 = (bf16[1024,4096]{1,0:T(8,128)(2,1)S(1)}, bf16[1024,4096]{1,0:T(8,128)(2,1)}, u32[]{:S(2)}) copy-start(bf16[1024,4096]{1,0:T(8,128)(2,1)} %fusion) | copy-start | bytes 25165828
  286.7 15.7 %slice-start = ((s8[8388608]{0:T(1024)(128)(4,1)}), s8[4194304]{0:T(1024)(128)(4,1)S(1)}, s32[]{:S(2)}) async-start(s8[8388608]{0:T(1024)(128)(4,1)} %bitcast.143), calls=%async_computation.5 | async-start | bytes 8388608
  296.4 6.1 slice-start.1
  331.4 160.5 %all-gather.9.cloned.1.call-start = ((), (), s32[]{:S(2)}) async-start(), calls=%async_computation.2 | async-start | bytes 5242880 | tf_op jit(solution)/shard_map/all_gather | solution.py:214
  331.4 7.6 collective-permute-start.14
  331.5 20.5 %collective-permute-start.10 = (bf16[512,4096]{1,0:T(8,128)(2,1)}, bf16[512,4096]{1,0:T(8,128)(2,1)}, u32[]{:S(2)}, u32[]{:S(2)}) collective-permute-start(bf16[512,4096]{1,0:T(8,128)(2,1)} %convolution_convert_fusion.1), channel_id=1, source_target_pairs={{0,8},{8,0},{16,24},{24,16},{1,9},{9,1},{17,25},{25,17},{2,10},{10... | collective-permute-start | bytes 12582920 | tf_op jit(solution)/shard_map/ppermute | solution.py:23
  332.0 389.5 %all-reduce.3.cloned.1.call-start = ((), (), s32[]{:S(2)}) async-start(), calls=%async_computation.4 | async-start | bytes 9437184 | tf_op jit(solution)/shard_map/psum | solution.py:89
  348.7 3.3 copy-start.6
  350.4 175.6 %collective-permute-start.15 = (bf16[256,4096]{1,0:T(8,128)(2,1)}, bf16[256,4096]{1,0:T(8,128)(2,1)}, u32[]{:S(2)}, u32[]{:S(2)}) collective-permute-start(bf16[256,4096]{1,0:T(8,128)(2,1)} %constant_dynamic-slice_fusion), channel_id=1, source_target_pairs={{0,16},{8,24},{16,0},{24,8},{1,17},{9,25},{17,1},{25,9},{2,18},{10... | collective-permute-start | bytes 6291464 | tf_op jit(solution)/shard_map/ppermute | solution.py:23
  360.9 2.0 copy-start.4
  362.9 48.2 %copy-start.15 = (s32[4096]{0:T(1024)S(1)}, s32[4096]{0:T(1024)}, u32[]{:S(2)}) copy-start(s32[4096]{0:T(1024)} %copy-done.14) | copy-start | bytes 49156
  362.9 48.2 %copy-start.17 = (s32[4096]{0:T(1024)S(1)}, s32[4096]{0:T(1024)}, u32[]{:S(2)}) copy-start(s32[4096]{0:T(1024)} %copy-done.16) | copy-start | bytes 49156
  364.5 169.2 %collective-permute-start.11 = (bf16[256,4096]{1,0:T(8,128)(2,1)}, bf16[256,4096]{1,0:T(8,128)(2,1)}, u32[]{:S(2)}, u32[]{:S(2)}) collective-permute-start(bf16[256,4096]{1,0:T(8,128)(2,1)} %constant_dynamic-slice_fusion.1), channel_id=1, source_target_pairs={{0,16},{8,24},{16,0},{24,8},{1,17},{9,25},{17,1},{25,9},{2,18},{10... | collective-permute-start | bytes 6291464 | tf_op jit(solution)/shard_map/ppermute | solution.py:23
  501.6 7.4 collective-permute-start.5
  525.9 4.6 collective-permute-start.6
  526.0 7.6 copy-start.5
  532.1 14.3 %collective-permute-start.7 = (bf16[1024,256]{1,0:T(8,128)(2,1)S(1)}, bf16[1024,256]{1,0:T(8,128)(2,1)S(1)}, u32[]{:S(2)}, u32[]{:S(2)}) collective-permute-start(bf16[1024,256]{1,0:T(8,128)(2,1)S(1)} %constant_dynamic-slice_fusion.2), channel_id=1, source_target_pairs={{0,16},{8,24},{16,0},{24,8},{1,17},{9,25},{17,1},{25,9},{2,18},{10... | collective-permute-start | bytes 1572872 | tf_op jit(solution)/shard_map/ppermute | solution.py:23
  721.5 47.6 %collective-permute-start.12 = (bf16[256,4096]{1,0:T(8,128)(2,1)}, bf16[256,4096]{1,0:T(8,128)(2,1)S(1)}, u32[]{:S(2)}, u32[]{:S(2)}) collective-permute-start(bf16[256,4096]{1,0:T(8,128)(2,1)} %get-tuple-element.13), channel_id=1, source_target_pairs={{0,16},{8,24},{16,0},{24,8},{1,17},{9,25},{17,1},{25,9},{2,18},{10... | collective-permute-start | bytes 6291464 | tf_op jit(solution)/shard_map/ppermute | solution.py:23
  723.0 58.8 %copy-start.8 = (bf16[256,4096]{1,0:T(8,128)(2,1)S(1)}, bf16[256,4096]{1,0:T(8,128)(2,1)}, u32[]{:S(2)}) copy-start(bf16[256,4096]{1,0:T(8,128)(2,1)} %get-tuple-element.13) | copy-start | bytes 6291460
  769.1 1.3 copy-start.9
  781.9 7.7 copy-start.7
  789.5 7.6 collective-permute-start.13
  789.6 48.1 %collective-permute-start.16 = (bf16[256,4096]{1,0:T(8,128)(2,1)S(1)}, bf16[256,4096]{1,0:T(8,128)(2,1)}, u32[]{:S(2)}, u32[]{:S(2)}) collective-permute-start(bf16[256,4096]{1,0:T(8,128)(2,1)S(1)} %copy-done.7), channel_id=1, source_target_pairs={{0,16},{8,24},{16,0},{24,8},{1,17},{9,25},{17,1},{25,9},{2,18},{10... | collective-permute-start | bytes 6291464 | tf_op jit(solution)/shard_map/ppermute | solution.py:23
  803.8 41.4 %copy-start.12 = (bf16[1024,256]{1,0:T(8,128)(2,1)S(1)}, bf16[1024,256]{1,0:T(8,128)(2,1)}, u32[]{:S(2)}) copy-start(bf16[1024,256]{1,0:T(8,128)(2,1)} %get-tuple-element.12) | copy-start | bytes 1572868
  803.8 56.2 %copy-start = (bf16[1024,4,128]{0,2,1:T(8,128)(2,1)S(1)}, bf16[1024,4,128]{0,2,1:T(8,128)(2,1)}, u32[]{:S(2)}) copy-start(bf16[1024,4,128]{0,2,1:T(8,128)(2,1)} %fusion.35) | copy-start | bytes 3145732
  845.2 16.1 %copy-start.1 = (bf16[1024,4,128]{0,2,1:T(8,128)(2,1)S(1)}, bf16[1024,4,128]{0,2,1:T(8,128)(2,1)}, u32[]{:S(2)}) copy-start(bf16[1024,4,128]{0,2,1:T(8,128)(2,1)} %fusion.33) | copy-start | bytes 3145732
  845.2 65.9 %collective-permute-start.17 = (bf16[512,4096]{1,0:T(8,128)(2,1)}, bf16[512,4096]{1,0:T(8,128)(2,1)}, u32[]{:S(2)}, u32[]{:S(2)}) collective-permute-start(bf16[512,4096]{1,0:T(8,128)(2,1)} %get-tuple-element.16), channel_id=1, source_target_pairs={{0,8},{8,0},{16,24},{24,16},{1,9},{9,1},{17,25},{25,17},{2,10},{10... | collective-permute-start | bytes 12582920 | tf_op jit(solution)/shard_map/ppermute | solution.py:23
  845.2 14.3 %collective-permute-start.8 = (bf16[1024,256]{1,0:T(8,128)(2,1)S(1)}, bf16[1024,256]{1,0:T(8,128)(2,1)S(1)}, u32[]{:S(2)}, u32[]{:S(2)}) collective-permute-start(bf16[1024,256]{1,0:T(8,128)(2,1)S(1)} %copy-done.12), channel_id=1, source_target_pairs={{0,16},{8,24},{16,0},{24,8},{1,17},{9,25},{17,1},{25,9},{2,18},{10... | collective-permute-start | bytes 1572872 | tf_op jit(solution)/shard_map/ppermute | solution.py:23
  859.9 36.6 %collective-permute-start.9 = (bf16[2048,256]{1,0:T(8,128)(2,1)S(1)}, bf16[2048,256]{1,0:T(8,128)(2,1)}, u32[]{:S(2)}, u32[]{:S(2)}) collective-permute-start(bf16[2048,256]{1,0:T(8,128)(2,1)S(1)} %maximum_select_fusion.4), channel_id=1, source_target_pairs={{0,8},{8,0},{16,24},{24,16},{1,9},{9,1},{17,25},{25,17},{2,10},{10... | collective-permute-start | bytes 3145736 | tf_op jit(solution)/shard_map/ppermute | solution.py:23
  861.8 3.0 copy-start.3
  861.8 3.0 copy-start.10
Sparse Core Ops, SparseCore 0:
  36.7 84.5 all-gather.4
  122.9 79.2 all-gather.6
  331.5 79.6 all-gather.10
  412.6 79.2 all-gather.8
  547.5 173.9 all-reduce.2
